TPU v7x, 512 devices: a whole 4x8x8 slice. The times are simulated.
512 devices in a mesh: span: 8 (over x, y_hi), seq: 64 (over y_lo, z, core).
Axes of the slice: x: 4, y: 8 (y_hi: 2, y_lo: 4; y = y_hi * 4 + y_lo), z: 8, core: 2. Of those that a mesh axis runs over, the one named last changes fastest.
Arguments:
- queries: bfloat16 [8, 1536, 4096], P('span', 'seq'), may hold values from -98 to 98
- key_rows: bfloat16 [8, 1536, 4096], P('span', 'seq'), may hold values from -4.1 to 4.1
- value_rows: bfloat16 [8, 1536, 4096], P('span', 'seq'), may hold values from -6 to 6
- block_mask: int32 [8, 8], replicated, may hold values from 0 to 1, as said below
- noise_level: int32 [8], replicated, may hold values from 0 to 7
- gate_table: float32 [8, 4096], replicated, may hold values from 2 to 16
Outputs:
- attended: bfloat16 [8, 1536, 4096], P('span', 'seq')
Inputs may be any that keep to these rules, and one draw needn't show every extreme that they name: block_mask[c][c] is 1 for every block c; block_mask[c][c2] is 0 where c2 > c or c2 < c - 2.
All inputs are finite; a program needn't handle non-finite values.
Results may differ from a plain program's by a relative error of at most 0.0065.
Values may be sent and summed in bfloat16 or wider, within the bound.
No kernel may reach another device: no remote copies, remote signals or barrier semaphores. Data moves between devices by JAX's collectives and lax.ppermute only.
A program may use at most 64 MiB of HBM per device.

v0:
```python
import math

import jax
import jax.numpy as jnp
from jax import lax
from jax.sharding import PartitionSpec as P

HD = 128
WINDOW = 2


def passed_along(block, axis, distance):
    devices = range(lax.axis_size(axis))
    route = [(i - distance, i) for i in devices if i - distance in devices]
    return lax.ppermute(block, axis, route)


def on_device(queries, key_rows, value_rows, block_mask, noise_level, gate_table):
    local_rows = queries.shape[1]
    features = queries.shape[2]
    head_count = features // HD
    group_size = lax.axis_size("seq")
    copies = max(1, group_size // head_count)
    slot_count = head_count * copies // group_size
    span_len = local_rows * group_size
    sub_rows = local_rows // copies
    query_rows = sub_rows * group_size
    position = lax.axis_index("seq")
    span_at = lax.axis_index("span")
    first_head = position * slot_count // copies
    scaling = HD ** (-0.5)
    query_block = math.gcd(query_rows, 512)
    key_block = math.gcd(span_len, 512)
    query_tiles_n = query_rows // query_block

    def spread(block):
        return jnp.repeat(block[0].reshape(local_rows, head_count, HD), copies, axis=1)

    def allowed(distance):
        column = span_at - distance
        return jnp.logical_and(column >= 0, block_mask[span_at, jnp.maximum(column, 0)] > 0)

    split_rows = queries[0].reshape(copies, sub_rows, head_count, HD)
    query_mine = lax.all_to_all(
        split_rows.transpose(1, 2, 0, 3).reshape(sub_rows, head_count * copies, HD),
        "seq",
        split_axis=1,
        concat_axis=0,
        tiled=True,
    )
    key_here = lax.all_to_all(spread(key_rows), "seq", split_axis=1, concat_axis=0, tiled=True)
    value_here = lax.all_to_all(spread(value_rows), "seq", split_axis=1, concat_axis=0, tiled=True)
    query_tiles = query_mine.reshape(query_tiles_n, query_block, slot_count, HD)
    running = (
        jnp.full((query_tiles_n, slot_count, query_block), -1e30, jnp.float32),
        jnp.zeros((query_tiles_n, slot_count, query_block), jnp.float32),
        jnp.zeros((query_tiles_n, slot_count, query_block, HD), jnp.float32),
    )

    def absorb(running, key_now, value_now, usable):
        key_tiles = key_now.reshape(span_len // key_block, key_block, slot_count, HD)
        value_tiles = value_now.reshape(span_len // key_block, key_block, slot_count, HD)

        def per_query(blocks):
            query_tile, maxima, totals, weighted = blocks

            def per_key(carry, tiles):
                maxima, totals, weighted = carry
                key_tile, value_tile = tiles
                scores = (
                    jnp.einsum(
                        "qph,kph->pqk", query_tile, key_tile, preferred_element_type=jnp.float32
                    )
                    * scaling
                )
                new_max = jnp.where(usable, jnp.maximum(maxima, scores.max(axis=-1)), maxima)
                expos = jnp.where(usable, jnp.exp(scores - new_max[..., None]), 0.0)
                shrink = jnp.exp(maxima - new_max)
                totals = totals * shrink + expos.sum(axis=-1)
                weighted = weighted * shrink[..., None] + jnp.einsum(
                    "pqk,kph->pqh",
                    expos.astype(jnp.bfloat16),
                    value_tile,
                    preferred_element_type=jnp.float32,
                )
                return ((new_max, totals, weighted), None)

            result, _ = lax.scan(per_key, (maxima, totals, weighted), (key_tiles, value_tiles))
            return result

        return lax.map(per_query, (query_tiles, running[0], running[1], running[2]))

    running = absorb(running, key_here, value_here, allowed(0))
    shifted = jnp.stack((key_here, value_here))
    for distance in range(1, WINDOW + 1):
        shifted = passed_along(shifted, "span", 1)
        running = absorb(running, shifted[0], shifted[1], allowed(distance))
    maxima, totals, weighted = running
    heard = weighted / totals[..., None]
    gate_row = lax.dynamic_index_in_dim(
        gate_table, noise_level[span_at], 0, keepdims=False
    ).reshape(head_count, HD)
    gate_mine = lax.dynamic_slice_in_dim(gate_row, first_head, slot_count, 0)
    gated = (heard * gate_mine[None, :, None, :]).astype(jnp.bfloat16)
    gated = gated.transpose(0, 2, 1, 3).reshape(query_rows, slot_count, HD)
    returned = lax.all_to_all(gated, "seq", split_axis=0, concat_axis=1, tiled=True)
    merged = returned.reshape(sub_rows, head_count, copies, HD).transpose(2, 0, 1, 3)
    return merged.reshape(1, local_rows, features)


def solution(mesh):
    in_specs = (
        P("span", "seq", None),
        P("span", "seq", None),
        P("span", "seq", None),
        P(),
        P(),
        P(),
    )
    out_specs = P("span", "seq", None)
    return jax.shard_map(
        on_device, mesh=mesh, in_specs=in_specs, out_specs=out_specs, check_vma=False
    )
```

profile of v0, /device:TPU:6, one launch (start us, length us, event | category | flops | bytes accessed | tf_op | source)
XLA Modules:
  0.0 184.9 jit_solution(4455109390114821184)
XLA Ops:
  0.0 1.0 copy.71
  1.0 0.8 copy.51
  1.8 14.5 %all-to-all-start = ((bf16[12,64,128]{2,0,1:T(8,128)(2,1)}), bf16[12,64,128]{2,0,1:T(8,128)(2,1)S(1)}, u32[]{:S(2)}, u32[]{:S(2)}) async-start(bf16[12,64,128]{2,0,1:T(8,128)(2,1)} %bitcast.34), calls=%async_computation | async-start | bytes 524288 | tf_op jit(solution)/shard_map/all_to_all | solution.py:44
  16.4 12.3 %all-to-all-done = bf16[12,64,128]{2,0,1:T(8,128)(2,1)S(1)} async-done(((bf16[12,64,128]{2,0,1:T(8,128)(2,1)}), bf16[12,64,128]{2,0,1:T(8,128)(2,1)S(1)}, u32[]{:S(2)}, u32[]{:S(2)}) %all-to-all-start) | async-done | bytes 196640 | tf_op jit(solution)/shard_map/all_to_all | solution.py:44
  28.8 0.8 broadcast_in_dim.51
  29.6 5.3 %all-to-all-start.1 = ((bf16[24,64,128]{2,0,1:T(8,128)(2,1)}), bf16[24,64,128]{2,0,1:T(8,128)(2,1)S(1)}, u32[]{:S(2)}, u32[]{:S(2)}) async-start(bf16[24,64,128]{2,0,1:T(8,128)(2,1)} %bitcast.39), calls=%async_computation.1 | async-start | bytes 786432 | tf_op jit(solution)/shard_map/all_to_all | solution.py:51
  35.0 14.4 %all-to-all-done.1 = bf16[24,64,128]{2,0,1:T(8,128)(2,1)S(1)} async-done(((bf16[24,64,128]{2,0,1:T(8,128)(2,1)}), bf16[24,64,128]{2,0,1:T(8,128)(2,1)S(1)}, u32[]{:S(2)}, u32[]{:S(2)}) %all-to-all-start.1) | async-done | bytes 393248 | tf_op jit(solution)/shard_map/all_to_all | solution.py:51
  49.4 0.8 broadcast_in_dim.52
  50.2 5.9 %all-to-all-start.2 = ((bf16[24,64,128]{2,0,1:T(8,128)(2,1)}), bf16[24,64,128]{2,0,1:T(8,128)(2,1)S(1)}, u32[]{:S(2)}, u32[]{:S(2)}) async-start(bf16[24,64,128]{2,0,1:T(8,128)(2,1)} %bitcast.44), calls=%async_computation.2 | async-start | bytes 786432 | tf_op jit(solution)/shard_map/all_to_all | solution.py:52
  56.2 0.6 copy-done.3
  56.8 0.6 dynamic_slice.74
  58.7 1.5 fusion.58
  62.7 7.9 %all-to-all-done.2 = bf16[24,64,128]{2,0,1:T(8,128)(2,1)S(1)} async-done(((bf16[24,64,128]{2,0,1:T(8,128)(2,1)}), bf16[24,64,128]{2,0,1:T(8,128)(2,1)S(1)}, u32[]{:S(2)}, u32[]{:S(2)}) %all-to-all-start.2) | async-done | bytes 393248 | tf_op jit(solution)/shard_map/all_to_all | solution.py:52
  70.6 1.0 pad_maximum_fusion
  71.6 5.0 %collective-permute-start = (bf16[2,1536,1,128]{3,1,2,0:T(8,128)(2,1)}, bf16[2,1536,1,128]{3,1,2,0:T(8,128)(2,1)S(1)}, u32[]{:S(2)}, u32[]{:S(2)}) collective-permute-start(bf16[2,1536,1,128]{3,1,2,0:T(8,128)(2,1)} %pad_maximum_fusion), channel_id=1, source_target_pairs={{0,64},{64,128},{128,192},{192,256},{256,320},{320,384},{384,448},... | collective-permute-start | bytes 2359304 | tf_op jit(solution)/shard_map/ppermute | solution.py:15
  76.7 7.1 %while.84 = (s32[]{:T(128)}, f32[3,1,256]{2,1,0:T(1,128)S(1)}, f32[3,1,256]{2,1,0:T(1,128)S(1)}, f32[3,1,256,128]{3,2,1,0:T(8,128)S(1)}, bf16[3,256,1,128]{3,1,2...) while((s32[]{:T(128)}, f32[3,1,256]{2,1,0:T(1,128)S(1)}, ...), condition=%wide.region_5.6_spmd, body=%wide.region_0.5_spmd.sunk | while | flops 68257280 | bytes 2576725 | solution.py:91
  76.8 2.3 %while.89 = (s32[]{:T(128)}, f32[1,256]{1,0:T(1,128)S(1)}, f32[1,256]{1,0:T(1,128)S(1)}, f32[1,256,128]{2,1,0:T(8,128)S(1)}, pred[]{:T(512)}, /*index=5*/bf16[3,...) while((s32[]{:T(128)}, f32[1,256]{1,0:T(1,128)S(1)}, ...), condition=%wide.region_4.4_spmd.clone, body=%wide.region_1.3_spmd.clone.sunk | while | flops 68257280 | bytes 2179196 | solution.py:88
  79.1 2.3 %while.89 = (s32[]{:T(128)}, f32[1,256]{1,0:T(1,128)S(1)}, f32[1,256]{1,0:T(1,128)S(1)}, f32[1,256,128]{2,1,0:T(8,128)S(1)}, pred[]{:T(512)}, /*index=5*/bf16[3,...) while((s32[]{:T(128)}, f32[1,256]{1,0:T(1,128)S(1)}, ...), condition=%wide.region_4.4_spmd.clone, body=%wide.region_1.3_spmd.clone.sunk | while | flops 68257280 | bytes 2179196 | solution.py:88
  81.5 2.3 %while.89 = (s32[]{:T(128)}, f32[1,256]{1,0:T(1,128)S(1)}, f32[1,256]{1,0:T(1,128)S(1)}, f32[1,256,128]{2,1,0:T(8,128)S(1)}, pred[]{:T(512)}, /*index=5*/bf16[3,...) while((s32[]{:T(128)}, f32[1,256]{1,0:T(1,128)S(1)}, ...), condition=%wide.region_4.4_spmd.clone, body=%wide.region_1.3_spmd.clone.sunk | while | flops 68257280 | bytes 2179196 | solution.py:88
  83.8 14.3 %collective-permute-done = bf16[2,1536,1,128]{3,1,2,0:T(8,128)(2,1)S(1)} collective-permute-done((bf16[2,1536,1,128]{3,1,2,0:T(8,128)(2,1)}, bf16[2,1536,1,128]{3,1,2,0:T(8,128)(2,1)S(1)}, u32[]{:S(2)}, u32[]{:S(2)}) %collective-permute-start) | collective-permute-done | bytes 786464 | tf_op jit(solution)/shard_map/ppermute | solution.py:15
  98.2 3.9 %collective-permute-start.1 = (bf16[2,1536,1,128]{3,1,2,0:T(8,128)(2,1)S(1)}, bf16[2,1536,1,128]{3,1,2,0:T(8,128)(2,1)}, u32[]{:S(2)}, u32[]{:S(2)}) collective-permute-start(bf16[2,1536,1,128]{3,1,2,0:T(8,128)(2,1)S(1)} %collective-permute-done), channel_id=1, source_target_pairs={{0,64},{64,128},{128,192},{192,256},{256,320},{320,384},{384,448},... | collective-permute-start | bytes 2359304 | tf_op jit(solution)/shard_map/ppermute | solution.py:15
  102.1 7.3 %while.86 = (s32[]{:T(128)}, f32[3,1,256]{2,1,0:T(1,128)S(1)}, f32[3,1,256]{2,1,0:T(1,128)S(1)}, f32[3,1,256,128]{3,2,1,0:T(8,128)S(1)}, f32[3,1,256]{2,1,0:T(1,...) while((s32[]{:T(128)}, f32[3,1,256]{2,1,0:T(1,128)S(1)}, ...), condition=%wide.region_11.12_spmd, body=%wide.region_6.11_spmd.sunk | while | flops 68223744 | bytes 2842965 | solution.py:91
  102.2 2.3 %while.90 = (s32[]{:T(128)}, f32[1,256]{1,0:T(1,128)S(1)}, f32[1,256]{1,0:T(1,128)S(1)}, f32[1,256,128]{2,1,0:T(8,128)S(1)}, pred[]{:T(512)}, /*index=5*/bf16[3,...) while((s32[]{:T(128)}, f32[1,256]{1,0:T(1,128)S(1)}, ...), condition=%wide.region_10.10_spmd, body=%wide.region_7.9_spmd.sunk | while | flops 68223744 | bytes 2179176 | solution.py:88
  102.7 0.3 fusion.90
  104.6 2.3 %while.90 = (s32[]{:T(128)}, f32[1,256]{1,0:T(1,128)S(1)}, f32[1,256]{1,0:T(1,128)S(1)}, f32[1,256,128]{2,1,0:T(8,128)S(1)}, pred[]{:T(512)}, /*index=5*/bf16[3,...) while((s32[]{:T(128)}, f32[1,256]{1,0:T(1,128)S(1)}, ...), condition=%wide.region_10.10_spmd, body=%wide.region_7.9_spmd.sunk | while | flops 68223744 | bytes 2179176 | solution.py:88
  105.1 0.3 fusion.90
  105.8 0.3 fusion.90
  106.6 0.3 fusion.90
  107.1 2.3 %while.90 = (s32[]{:T(128)}, f32[1,256]{1,0:T(1,128)S(1)}, f32[1,256]{1,0:T(1,128)S(1)}, f32[1,256,128]{2,1,0:T(8,128)S(1)}, pred[]{:T(512)}, /*index=5*/bf16[3,...) while((s32[]{:T(128)}, f32[1,256]{1,0:T(1,128)S(1)}, ...), condition=%wide.region_10.10_spmd, body=%wide.region_7.9_spmd.sunk | while | flops 68223744 | bytes 2179176 | solution.py:88
  107.5 0.3 fusion.90
  109.0 0.3 fusion.90
  109.4 24.2 %collective-permute-done.1 = bf16[2,1536,1,128]{3,1,2,0:T(8,128)(2,1)} collective-permute-done((bf16[2,1536,1,128]{3,1,2,0:T(8,128)(2,1)S(1)}, bf16[2,1536,1,128]{3,1,2,0:T(8,128)(2,1)}, u32[]{:S(2)}, u32[]{:S(2)}) %collective-permute-start.1) | collective-permute-done | bytes 786464 | tf_op jit(solution)/shard_map/ppermute | solution.py:15
  133.6 1.2 fusion.56
  134.8 7.3 %while.88 = (s32[]{:T(128)}, f32[3,1,256]{2,0,1:T(4,128)S(1)}, f32[3,1,256,128]{3,2,1,0:T(8,128)S(1)}, f32[3,1,256]{2,1,0:T(1,128)S(1)}, f32[3,1,256]{2,1,0:T(1,...) while((s32[]{:T(128)}, f32[3,1,256]{2,0,1:T(4,128)S(1)}, ...), condition=%wide.region_17.18_spmd, body=%wide.region_12.17_spmd.sunk | while | flops 68223744 | bytes 2840905 | solution.py:91
  134.9 2.3 %while.91 = (s32[]{:T(128)}, f32[1,256]{1,0:T(1,128)S(1)}, f32[1,256]{1,0:T(1,128)S(1)}, f32[1,256,128]{2,1,0:T(8,128)S(1)}, pred[]{:T(512)}, /*index=5*/bf16[3,...) while((s32[]{:T(128)}, f32[1,256]{1,0:T(1,128)S(1)}, ...), condition=%wide.region_16.16_spmd, body=%wide.region_13.15_spmd.sunk | while | flops 68223744 | bytes 2179176 | solution.py:88
  135.3 0.3 fusion.85
  136.8 0.3 fusion.85
  137.3 2.3 %while.91 = (s32[]{:T(128)}, f32[1,256]{1,0:T(1,128)S(1)}, f32[1,256]{1,0:T(1,128)S(1)}, f32[1,256,128]{2,1,0:T(8,128)S(1)}, pred[]{:T(512)}, /*index=5*/bf16[3,...) while((s32[]{:T(128)}, f32[1,256]{1,0:T(1,128)S(1)}, ...), condition=%wide.region_16.16_spmd, body=%wide.region_13.15_spmd.sunk | while | flops 68223744 | bytes 2179176 | solution.py:88
  137.8 0.3 fusion.85
  138.5 0.3 fusion.85
  139.3 0.3 fusion.85
  139.7 2.3 %while.91 = (s32[]{:T(128)}, f32[1,256]{1,0:T(1,128)S(1)}, f32[1,256]{1,0:T(1,128)S(1)}, f32[1,256,128]{2,1,0:T(8,128)S(1)}, pred[]{:T(512)}, /*index=5*/bf16[3,...) while((s32[]{:T(128)}, f32[1,256]{1,0:T(1,128)S(1)}, ...), condition=%wide.region_16.16_spmd, body=%wide.region_13.15_spmd.sunk | while | flops 68223744 | bytes 2179176 | solution.py:88
  140.2 0.3 fusion.85
  142.3 0.5 broadcast.107
  142.8 0.8 reduce.19
  143.6 39.0 %all_to_all.60 = bf16[64,2,768]{2,1,0:T(2,128)(2,1)S(1)} all-to-all(bf16[64,2,768]{2,1,0:T(2,128)(2,1)S(1)} %reshape.143), channel_id=1, replica_groups=mesh['span'=8,'seq'=64] {'seq'}, dimensions={0} | all-to-all | bytes 393216 | tf_op jit(solution)/shard_map/all_to_all | solution.py:106
  182.8 1.2 reduce.18
  184.1 0.8 reshape.138
  (230 shorter events, 17.2 us)
Async XLA Ops:
  0.0 62.6 %copy-start = (f32[8,4096]{1,0:T(8,128)S(1)}, f32[8,4096]{1,0:T(8,128)}, u32[]{:S(2)}) copy-start(f32[8,4096]{1,0:T(8,128)} %param.23) | copy-start | bytes 393220
  1.8 14.5 %copy-start.1 = (bf16[1,24,4096]{2,1,0:T(8,128)(2,1)S(1)}, bf16[1,24,4096]{2,1,0:T(8,128)(2,1)}, u32[]{:S(2)}) copy-start(bf16[1,24,4096]{2,1,0:T(8,128)(2,1)} %param.19) | copy-start | bytes 589828
  1.8 27.0 %all-to-all-start = ((bf16[12,64,128]{2,0,1:T(8,128)(2,1)}), bf16[12,64,128]{2,0,1:T(8,128)(2,1)S(1)}, u32[]{:S(2)}, u32[]{:S(2)}) async-start(bf16[12,64,128]{2,0,1:T(8,128)(2,1)} %bitcast.34), calls=%async_computation | async-start | bytes 524288 | tf_op jit(solution)/shard_map/all_to_all | solution.py:44
  29.6 5.3 %copy-start.2 = (bf16[1,24,4096]{2,1,0:T(8,128)(2,1)S(1)}, bf16[1,24,4096]{2,1,0:T(8,128)(2,1)}, u32[]{:S(2)}) copy-start(bf16[1,24,4096]{2,1,0:T(8,128)(2,1)} %param.20) | copy-start | bytes 589828
  29.6 19.8 %all-to-all-start.1 = ((bf16[24,64,128]{2,0,1:T(8,128)(2,1)}), bf16[24,64,128]{2,0,1:T(8,128)(2,1)S(1)}, u32[]{:S(2)}, u32[]{:S(2)}) async-start(bf16[24,64,128]{2,0,1:T(8,128)(2,1)} %bitcast.39), calls=%async_computation.1 | async-start | bytes 786432 | tf_op jit(solution)/shard_map/all_to_all | solution.py:51
  50.2 20.4 %all-to-all-start.2 = ((bf16[24,64,128]{2,0,1:T(8,128)(2,1)}), bf16[24,64,128]{2,0,1:T(8,128)(2,1)S(1)}, u32[]{:S(2)}, u32[]{:S(2)}) async-start(bf16[24,64,128]{2,0,1:T(8,128)(2,1)} %bitcast.44), calls=%async_computation.2 | async-start | bytes 786432 | tf_op jit(solution)/shard_map/all_to_all | solution.py:52
  56.2 0.7 copy-start.3
  71.6 26.5 %collective-permute-start = (bf16[2,1536,1,128]{3,1,2,0:T(8,128)(2,1)}, bf16[2,1536,1,128]{3,1,2,0:T(8,128)(2,1)S(1)}, u32[]{:S(2)}, u32[]{:S(2)}) collective-permute-start(bf16[2,1536,1,128]{3,1,2,0:T(8,128)(2,1)} %pad_maximum_fusion), channel_id=1, source_target_pairs={{0,64},{64,128},{128,192},{192,256},{256,320},{320,384},{384,448},... | collective-permute-start | bytes 2359304 | tf_op jit(solution)/shard_map/ppermute | solution.py:15
  98.2 35.4 %collective-permute-start.1 = (bf16[2,1536,1,128]{3,1,2,0:T(8,128)(2,1)S(1)}, bf16[2,1536,1,128]{3,1,2,0:T(8,128)(2,1)}, u32[]{:S(2)}, u32[]{:S(2)}) collective-permute-start(bf16[2,1536,1,128]{3,1,2,0:T(8,128)(2,1)S(1)} %collective-permute-done), channel_id=1, source_target_pairs={{0,64},{64,128},{128,192},{192,256},{256,320},{320,384},{384,448},... | collective-permute-start | bytes 2359304 | tf_op jit(solution)/shard_map/ppermute | solution.py:15
where the time goes:
time: 186 us; the launch traced here: 185 us
  waiting for transfers between devices  73.2 us (39%)
  blocking collectives  39 us (21%)
  starting transfers between devices  34.6 us (19%)
  matrix products  15.2 us (8%)
  local copies, waits for them, and re-layouts  10.1 us (5%)
  other arithmetic  7.09 us (4%)
  between operations  4 us (2%)
    all_to_all x1, blocking collectives, on_device(): lax.all_to_all(gated, 'seq', split_axis=0, concat_axis=1, tiled=True)  39 us
    ppermute x2, waiting for transfers between devices, passed_along(): return lax.ppermute(block, axis, route)  38.6 us
    all_to_all x1, starting transfers between devices, on_device(): lax.all_to_all(split_rows.transpose(1, 2, 0, 3).reshape(sub_rows, head_co...  14.5 us
    all_to_all x1, waiting for transfers between devices, on_device(): lax.all_to_all(spread(key_rows), 'seq', split_axis=1, concat_axis=0, tile...  14.4 us
    all_to_all x1, waiting for transfers between devices, on_device(): lax.all_to_all(split_rows.transpose(1, 2, 0, 3).reshape(sub_rows, head_co...  12.3 us
    ppermute x2, starting transfers between devices, passed_along(): return lax.ppermute(block, axis, route)  8.9 us
    dot_general x27, matrix products, per_key(): jnp.einsum('pqk,kph->pqh', expos.astype(jnp.bfloat16), value_tile, prefer...  8.22 us
    all_to_all x1, waiting for transfers between devices, on_device(): lax.all_to_all(spread(value_rows), 'seq', split_axis=1, concat_axis=0, ti...  7.94 us
  transfers between devices with their start and end apart: 5, of which 5 were waited for; matrix products, arithmetic and copies ran while one was open for 8% of the time, Pallas kernels for 0%

commit v1 on v0

v1 whole, which is shorter than its diff:
```python
import functools

import jax
import jax.numpy as jnp
from jax import lax
from jax.experimental import pallas as pl
from jax.experimental.pallas import tpu as pltpu
from jax.sharding import PartitionSpec as P

HD = 128
WINDOW = 2
LOG2E = 1.4426950408889634
VMEM_LIMIT = 48 * 1024 * 1024


def attend(first, last, scale, flag_ref, q_ref, kv_ref, kvx_ref, *rest):
    if first:
        state_in = None
    else:
        state_in, rest = rest[:3], rest[3:]
    if last:
        gate_ref, out_ref = rest
    else:
        m_out, l_out, a_out = rest
    rows = q_ref.shape[0]
    tile = min(256, rows)
    const = scale * LOG2E

    def whole(t, with_keys):
        at = pl.ds(t * tile, tile)
        if with_keys:
            q = q_ref[at, :]
            dims = (((1,), (1,)), ((), ()))
            scores = [
                lax.dot_general(q, ref[0], dims, preferred_element_type=jnp.float32)
                for ref in (kv_ref, kvx_ref)
            ]
            top = jnp.maximum(scores[0].max(axis=1, keepdims=True), scores[1].max(axis=1, keepdims=True))
            if not first:
                before = state_in[0][at, :1]
                top = jnp.maximum(top, before)
            expos = [jnp.exp2((s - top) * const) for s in scores]
            total = expos[0].sum(axis=1, keepdims=True) + expos[1].sum(axis=1, keepdims=True)
            heard = sum(
                jnp.dot(e.astype(jnp.bfloat16), ref[1], preferred_element_type=jnp.float32)
                for e, ref in zip(expos, (kv_ref, kvx_ref))
            )
            if not first:
                shrink = jnp.exp2((before - top) * const)
                total = total + state_in[1][at, :1] * shrink
                heard = heard + state_in[2][at, :] * shrink
        else:
            top, total, heard = state_in[0][at, :1], state_in[1][at, :1], state_in[2][at, :]
        if last:
            out_ref[at, :] = (heard / total * gate_ref[...]).astype(jnp.bfloat16)
        else:
            m_out[at, :] = jnp.broadcast_to(top, (tile, HD))
            l_out[at, :] = jnp.broadcast_to(total, (tile, HD))
            a_out[at, :] = heard

    def run(with_keys):
        for t in range(rows // tile):
            whole(t, with_keys)

    if first:
        run(True)
    else:
        usable = flag_ref[0] > 0

        @pl.when(usable)
        def _():
            run(True)

        @pl.when(jnp.logical_not(usable))
        def _():
            run(False)


def step(flag, q, kv, kvx, state=None, gate=None):
    first, last = state is None, gate is not None
    rows, keys = q.shape[0], 2 * kv.shape[1]
    vmem = pl.BlockSpec(memory_space=pltpu.VMEM)
    operands = [flag, q, kv, kvx] + list(state or ()) + ([gate] if last else [])
    in_specs = [pl.BlockSpec(memory_space=pltpu.SMEM)] + [vmem] * (len(operands) - 1)
    stat = jax.ShapeDtypeStruct((rows, HD), jnp.float32)
    out_shape = jax.ShapeDtypeStruct((rows, HD), jnp.bfloat16) if last else (stat, stat, stat)
    return pl.pallas_call(
        functools.partial(attend, first, last, HD ** -0.5),
        out_shape=out_shape,
        in_specs=in_specs,
        out_specs=vmem if last else (vmem,) * 3,
        compiler_params=pltpu.CompilerParams(vmem_limit_bytes=VMEM_LIMIT),
        cost_estimate=pl.CostEstimate(
            flops=4 * rows * keys * HD, bytes_accessed=4 * rows * HD * 8, transcendentals=rows * keys
        ),
    )(*operands)


def on_device(queries, key_rows, value_rows, block_mask, noise_level, gate_table):
    local = queries.shape[1]
    heads = queries.shape[2] // HD
    group = lax.axis_size("seq")
    spans = lax.axis_size("span")
    cores = group // heads
    chips = [[h * cores + c for h in range(heads)] for c in range(cores)]
    rows = heads * local
    position = lax.axis_index("seq")
    span_at = lax.axis_index("span")
    head = position // cores

    def exchange(block):
        return lax.all_to_all(
            block, "seq", split_axis=0, concat_axis=0, axis_index_groups=chips, tiled=True
        )

    def from_earlier(block, distance):
        return lax.ppermute(block, "span", [(i, i + distance) for i in range(spans - distance)])

    def other_core(block):
        return lax.ppermute(block, "seq", [(i, i ^ 1) for i in range(group)])

    def allowed(distance):
        column = span_at - distance
        usable = jnp.logical_and(column >= 0, block_mask[span_at, jnp.maximum(column, 0)] > 0)
        return usable.astype(jnp.int32).reshape(1)

    mixed = jnp.concatenate((queries[0], key_rows[0], value_rows[0]), axis=0)
    mixed = mixed.reshape(3 * local, heads, HD).transpose(1, 0, 2)
    got = exchange(mixed)
    q = got[:, :local].reshape(rows, HD)
    kv = got[:, local:].reshape(heads, 2, local, HD).transpose(1, 0, 2, 3).reshape(2, rows, HD)

    kv1 = from_earlier(kv, 1)
    kv2 = from_earlier(kv, 2)
    kvx = other_core(kv)
    state = step(allowed(0), q, kv, kvx)
    kv2x = other_core(kv2)
    state = step(allowed(2), q, kv2, kv2x, state)
    kv1x = other_core(kv1)
    gate_row = lax.dynamic_slice(
        gate_table, (noise_level[span_at], head * HD), (1, HD)
    )
    out = step(allowed(1), q, kv1, kv1x, state, gate_row)

    back = exchange(out.reshape(heads, local, HD))
    return back.transpose(1, 0, 2).reshape(1, local, heads * HD)


def solution(mesh):
    in_specs = (
        P("span", "seq", None),
        P("span", "seq", None),
        P("span", "seq", None),
        P(),
        P(),
        P(),
    )
    out_specs = P("span", "seq", None)
    return jax.shard_map(
        on_device, mesh=mesh, in_specs=in_specs, out_specs=out_specs, check_vma=False
    )
```

time: 186 us -> 97.5 us (0.52)
  waiting for transfers between devices: 73.2 us -> 10.9 us
  starting transfers between devices: 34.6 us -> 12.6 us
  blocking collectives: 39 us -> 54.3 us
  matrix products: 15.2 us -> 0 us
  Pallas kernels: 0 us -> 7.23 us
  other arithmetic: 7.09 us -> 0.07 us
  local copies, waits for them, and re-layouts: 10.1 us -> 6.55 us
    all_to_all x3 -> x0, waiting for transfers between devices: 34.7 us -> none  [the longest x1 14.4 us: on_device(): lax.all_to_all(spread(key_rows), 'seq', split_axis=1, concat_axis=0, tile...]
    ppermute x2 -> x5, waiting for transfers between devices: 38.6 us -> 10.9 us  [the longest x2 10.8 us: from_earlier(): lax.ppermute(block, 'span', [(i, i + distance) for i in range(spans - dis...]
    all_to_all x3 -> x0, starting transfers between devices: 25.7 us -> none  [the longest x1 14.5 us: on_device(): lax.all_to_all(split_rows.transpose(1, 2, 0, 3).reshape(sub_rows, head_co...]
    all_to_all x1 -> x2, blocking collectives: 39 us -> 54.3 us  [exchange(): lax.all_to_all(block, 'seq', split_axis=0, concat_axis=0, axis_index_grou...]
    dot_general x54 -> x0, matrix products: 15.2 us -> none  [the longest x27 8.22 us: per_key(): jnp.einsum('pqk,kph->pqh', expos.astype(jnp.bfloat16), value_tile, prefer...]
    pallas_call x0 -> x3, Pallas kernels: none -> 7.23 us  [step(): pl.pallas_call(functools.partial(attend, first, last, HD ** (-0.5)), out_...]
    ppermute x2 -> x5, starting transfers between devices: 8.9 us -> 12.6 us  [the longest x2 6.37 us: from_earlier(): lax.ppermute(block, 'span', [(i, i + distance) for i in range(spans - dis...]
    reduce_sum x27 -> x0, other arithmetic: 3.42 us -> none  [per_key(): totals = totals * shrink + expos.sum(axis=-1)]
  transfers between devices with their start and end apart: 5 -> 5, of which waited for: 5 -> 1; matrix products, arithmetic and copies ran while one was open for 8% -> 3% of each run, Pallas kernels for 0% -> 5%
where the time goes in v1:
time: 97.5 us; the launch traced here: 95.6 us
  blocking collectives  54.3 us (56%)
  starting transfers between devices  12.6 us (13%)
  waiting for transfers between devices  10.9 us (11%)
  Pallas kernels  7.23 us (7%)
  local copies, waits for them, and re-layouts  6.55 us (7%)
  between operations  4.02 us (4%)
    all_to_all x2, blocking collectives, exchange(): lax.all_to_all(block, 'seq', split_axis=0, concat_axis=0, axis_index_grou...  54.3 us
    ppermute x2, waiting for transfers between devices, from_earlier(): lax.ppermute(block, 'span', [(i, i + distance) for i in range(spans - dis...  10.8 us
    pallas_call x3, Pallas kernels, step(): pl.pallas_call(functools.partial(attend, first, last, HD ** (-0.5)), out_...  7.23 us
    ppermute x2, starting transfers between devices, from_earlier(): lax.ppermute(block, 'span', [(i, i + distance) for i in range(spans - dis...  6.37 us
    ppermute x3, starting transfers between devices, other_core(): return lax.ppermute(block, 'seq', [(i, i ^ 1) for i in range(group)])  6.24 us
    unnamed x9, local copies, waits for them, and re-layouts  2.61 us
  transfers between devices with their start and end apart: 5, of which 1 were waited for; matrix products, arithmetic and copies ran while one was open for 3% of the time, Pallas kernels for 5%

profile of v1, /device:TPU:6, one launch (start us, length us, event | category | flops | bytes accessed | tf_op | source)
XLA Modules:
  0.0 95.6 jit_solution(6674273870822302438)
XLA Ops:
  0.0 0.0 copy-start
  0.0 1.0 %copy.20 = bf16[3,8,32,128]{3,2,1,0:T(8,128)(2,1)S(1)} copy(bf16[3,8,32,128]{3,1,2,0:T(8,128)(2,1)} %bitcast.38) | data formatting | bytes 393216
  1.0 0.0 copy-done
  1.0 0.0 copy-start.1
  1.1 0.9 copy-done.1
  2.0 0.1 maximum_bitcast_fusion
  2.1 0.2 copy.17
  2.3 31.5 %all_to_all.10 = bf16[32,72,128]{2,1,0:T(8,128)(2,1)S(1)} all-to-all(bf16[32,72,128]{2,1,0:T(8,128)(2,1)S(1)} %copy.17), channel_id=1, replica_groups={{0,2,4,6,8,10,12,14,16,18,20,22,24,26,28,30,32,34,36,38,40,42,44,46,48,..., dimensions={0} | all-to-all | bytes 1179648 | tf_op jit(solution)/shard_map/all_to_all | solution.py:112
  33.9 1.3 %collective-permute-start.2 = (bf16[2,768,128]{2,1,0:T(8,128)(2,1)S(1)}, bf16[2,768,128]{2,1,0:T(8,128)(2,1)S(1)}, u32[]{:S(2)}, u32[]{:S(2)}) collective-permute-start(bf16[2,768,128]{2,1,0:T(8,128)(2,1)S(1)} %bitcast.29), channel_id=1, source_target_pairs={{0,128},{64,192},{128,256},{192,320},{256,384},{320,448},{1,129},{... | collective-permute-start | bytes 1179656 | tf_op jit(solution)/shard_map/ppermute | solution.py:117
  35.2 5.1 %collective-permute-start = (bf16[2,768,128]{2,1,0:T(8,128)(2,1)S(1)}, bf16[2,768,128]{2,1,0:T(8,128)(2,1)S(1)}, u32[]{:S(2)}, u32[]{:S(2)}) collective-permute-start(bf16[2,768,128]{2,1,0:T(8,128)(2,1)S(1)} %bitcast.30), channel_id=1, source_target_pairs={{0,64},{64,128},{128,192},{192,256},{256,320},{320,384},{384,448},... | collective-permute-start | bytes 1179656 | tf_op jit(solution)/shard_map/ppermute | solution.py:117
  40.3 1.9 %collective-permute-start.4 = (bf16[2,768,128]{2,1,0:T(8,128)(2,1)S(1)}, bf16[2,768,128]{2,1,0:T(8,128)(2,1)S(1)}, u32[]{:S(2)}, u32[]{:S(2)}) collective-permute-start(bf16[2,768,128]{2,1,0:T(8,128)(2,1)S(1)} %bitcast.31), channel_id=1, source_target_pairs={{0,1},{1,0},{2,3},{3,2},{4,5},{5,4},{6,7},{7,6},{8,9},{9,8},{10,11... | collective-permute-start | bytes 1179656 | tf_op jit(solution)/shard_map/ppermute | solution.py:120
  42.2 10.8 %collective-permute-done.2.kv_ref = bf16[2,768,128]{2,1,0:T(8,128)(2,1)S(1)} collective-permute-done((bf16[2,768,128]{2,1,0:T(8,128)(2,1)S(1)}, bf16[2,768,128]{2,1,0:T(8,128)(2,1)S(1)}, u32[]{:S(2)}, u32[]{:S(2)}) %collective-permute-start.2) | collective-permute-done | bytes 393248 | tf_op jit(solution)/shard_map/ppermute | solution.py:117
  53.0 1.9 %collective-permute-start.3 = (bf16[2,768,128]{2,1,0:T(8,128)(2,1)S(1)}, bf16[2,768,128]{2,1,0:T(8,128)(2,1)S(1)}, u32[]{:S(2)}, u32[]{:S(2)}) collective-permute-start(bf16[2,768,128]{2,1,0:T(8,128)(2,1)S(1)} %collective-permute-done.2.kv_ref), channel_id=1, source_target_pairs={{0,1},{1,0},{2,3},{3,2},{4,5},{5,4},{6,7},{7,6},{8,9},{9,8},{10,11... | collective-permute-start | bytes 1179656 | tf_op jit(solution)/shard_map/ppermute | solution.py:120
  55.0 0.0 collective-permute-done.kv_ref
  55.0 2.4 %collective-permute-start.1 = (bf16[2,768,128]{2,1,0:T(8,128)(2,1)S(1)}, bf16[2,768,128]{2,1,0:T(8,128)(2,1)S(1)}, u32[]{:S(2)}, u32[]{:S(2)}) collective-permute-start(bf16[2,768,128]{2,1,0:T(8,128)(2,1)S(1)} %collective-permute-done.kv_ref), channel_id=1, source_target_pairs={{0,1},{1,0},{2,3},{3,2},{4,5},{5,4},{6,7},{7,6},{8,9},{9,8},{10,11... | collective-permute-start | bytes 1179656 | tf_op jit(solution)/shard_map/ppermute | solution.py:120
  57.4 0.0 copy-start.2
  57.4 0.6 copy-done.2
  58.1 0.6 dynamic_slice.18
  59.9 1.5 %fusion = (s32[1,1]{1,0:T(1,128)}, s32[1,1]{1,0:T(1,128)}, s32[1,1]{1,0:T(1,128)}) fusion(s32[8,8]{1,0:T(8,128)} %param.9, s32[]{:T(128)S(6)} %select_n.20, s32[]{:T(128)S(6)} %max.11, s32[]{:T(128)S(6)} %max.9, s32[]{:T(128)S(6)} %max.10), kind=kLoop, calls=%fused_computation.1 | loop fusion | bytes 40 | tf_op jit(solution)/shard_map/dynamic_slice | solution.py:124
  64.0 0.8 dynamic_slice.19.rest_3_
  64.8 0.0 collective-permute-done.4.kvx_ref
  64.8 2.1 %shard_map.64 = (f32[768,128]{1,0:T(8,128)S(1)}, f32[768,128]{1,0:T(8,128)S(1)}, f32[768,128]{1,0:T(8,128)S(1)}) custom-call(s32[1]{0:T(128)} %bitcast.10.flag_ref, bf16[768,128]{1,0:T(8,128)(2,1)S(1)} %bitcast.25, bf16[2,768,128]{2,1,0:T(8,128)(2,1)S(1)} %bitcast.32, bf16[2,768,128]{2,1,0:T(8,128)(2,1)S(1)} %collective-permute-done.4.kvx_ref), custom_call_target="tpu_custom_call" | custom-call | flops 603979776 | bytes 3145728 | tf_op jit(solution)/shard_map/pallas_call | solution.py:87
  66.8 0.0 collective-permute-done.3.kvx_ref
  66.8 2.6 %shard_map.65 = (f32[768,128]{1,0:T(8,128)S(1)}, f32[768,128]{1,0:T(8,128)S(1)}, f32[768,128]{1,0:T(8,128)S(1)}) custom-call(s32[1]{0:T(128)} %bitcast.8.flag_ref, bf16[768,128]{1,0:T(8,128)(2,1)S(1)} %bitcast.26, bf16[2,768,128]{2,1,0:T(8,128)(2,1)S(1)} %collective-permute-done.2.kv_ref, bf16[2,768,128]{2,1,0:T(8,128)(2,1)S(1)} %collective-permute-done.3.kvx_ref, ...), custom_call_target="tpu_custom_call" | custom-call | flops 603979776 | bytes 3145728 | tf_op jit(solution)/shard_map/pallas_call | solution.py:87
  69.4 0.0 collective-permute-done.1.kvx_ref
  69.4 2.6 %shard_map.66 = bf16[768,128]{1,0:T(8,128)(2,1)S(1)} custom-call(s32[1]{0:T(128)} %bitcast.1.flag_ref, bf16[768,128]{1,0:T(8,128)(2,1)S(1)} %bitcast.27, bf16[2,768,128]{2,1,0:T(8,128)(2,1)S(1)} %collective-permute-done.kv_ref, bf16[2,768,128]{2,1,0:T(8,128)(2,1)S(1)} %collective-permute-done.1.kvx_ref, f32[768,128]{1,0:T(8,128)S(1)} %get-tuple-element.14.rest_0_, ...), custom_call_target="tpu_custom_call" | custom-call | flops 603979776 | bytes 3145728 | tf_op jit(solution)/shard_map/pallas_call | solution.py:87
  72.0 22.8 %all_to_all.11 = bf16[32,24,128]{2,1,0:T(8,128)(2,1)S(1)} all-to-all(bf16[32,24,128]{2,1,0:T(8,128)(2,1)S(1)} %bitcast.28), channel_id=1, replica_groups={{0,2,4,6,8,10,12,14,16,18,20,22,24,26,28,30,32,34,36,38,40,42,44,46,48,..., dimensions={0} | all-to-all | bytes 393216 | tf_op jit(solution)/shard_map/all_to_all | solution.py:112
  94.9 0.8 reshape.53
  (6 shorter events, 0.2 us)
Async XLA Ops:
  0.0 1.0 %copy-start = (bf16[1,24,4096]{2,1,0:T(8,128)(2,1)S(1)}, bf16[1,24,4096]{2,1,0:T(8,128)(2,1)}, u32[]{:S(2)}) copy-start(bf16[1,24,4096]{2,1,0:T(8,128)(2,1)} %param.7) | copy-start | bytes 589828
  1.0 0.9 copy-start.1
  33.9 19.2 %collective-permute-start.2 = (bf16[2,768,128]{2,1,0:T(8,128)(2,1)S(1)}, bf16[2,768,128]{2,1,0:T(8,128)(2,1)S(1)}, u32[]{:S(2)}, u32[]{:S(2)}) collective-permute-start(bf16[2,768,128]{2,1,0:T(8,128)(2,1)S(1)} %bitcast.29), channel_id=1, source_target_pairs={{0,128},{64,192},{128,256},{192,320},{256,384},{320,448},{1,129},{... | collective-permute-start | bytes 1179656 | tf_op jit(solution)/shard_map/ppermute | solution.py:117
  35.2 19.8 %collective-permute-start = (bf16[2,768,128]{2,1,0:T(8,128)(2,1)S(1)}, bf16[2,768,128]{2,1,0:T(8,128)(2,1)S(1)}, u32[]{:S(2)}, u32[]{:S(2)}) collective-permute-start(bf16[2,768,128]{2,1,0:T(8,128)(2,1)S(1)} %bitcast.30), channel_id=1, source_target_pairs={{0,64},{64,128},{128,192},{192,256},{256,320},{320,384},{384,448},... | collective-permute-start | bytes 1179656 | tf_op jit(solution)/shard_map/ppermute | solution.py:117
  40.3 24.5 %collective-permute-start.4 = (bf16[2,768,128]{2,1,0:T(8,128)(2,1)S(1)}, bf16[2,768,128]{2,1,0:T(8,128)(2,1)S(1)}, u32[]{:S(2)}, u32[]{:S(2)}) collective-permute-start(bf16[2,768,128]{2,1,0:T(8,128)(2,1)S(1)} %bitcast.31), channel_id=1, source_target_pairs={{0,1},{1,0},{2,3},{3,2},{4,5},{5,4},{6,7},{7,6},{8,9},{9,8},{10,11... | collective-permute-start | bytes 1179656 | tf_op jit(solution)/shard_map/ppermute | solution.py:120
  53.0 13.8 %collective-permute-start.3 = (bf16[2,768,128]{2,1,0:T(8,128)(2,1)S(1)}, bf16[2,768,128]{2,1,0:T(8,128)(2,1)S(1)}, u32[]{:S(2)}, u32[]{:S(2)}) collective-permute-start(bf16[2,768,128]{2,1,0:T(8,128)(2,1)S(1)} %collective-permute-done.2.kv_ref), channel_id=1, source_target_pairs={{0,1},{1,0},{2,3},{3,2},{4,5},{5,4},{6,7},{7,6},{8,9},{9,8},{10,11... | collective-permute-start | bytes 1179656 | tf_op jit(solution)/shard_map/ppermute | solution.py:120
  55.0 14.5 %collective-permute-start.1 = (bf16[2,768,128]{2,1,0:T(8,128)(2,1)S(1)}, bf16[2,768,128]{2,1,0:T(8,128)(2,1)S(1)}, u32[]{:S(2)}, u32[]{:S(2)}) collective-permute-start(bf16[2,768,128]{2,1,0:T(8,128)(2,1)S(1)} %collective-permute-done.kv_ref), channel_id=1, source_target_pairs={{0,1},{1,0},{2,3},{3,2},{4,5},{5,4},{6,7},{7,6},{8,9},{9,8},{10,11... | collective-permute-start | bytes 1179656 | tf_op jit(solution)/shard_map/ppermute | solution.py:120
  57.4 0.7 copy-start.2

commit v2 on v1

v2 whole, which is shorter than its diff:
```python
import functools

import jax
import jax.numpy as jnp
from jax import lax
from jax.experimental import pallas as pl
from jax.experimental.pallas import tpu as pltpu
from jax.sharding import Mesh
from jax.sharding import PartitionSpec as P

HD = 128
SPAN = ("x", "y_hi")
CHIPS = ("y_lo", "z")
CONST = HD ** (-0.5) * 1.4426950408889634
TILE = 384
VMEM_LIMIT = 48 * 1024 * 1024


def weigh(q, halves, top, const):
    dims = (((1,), (1,)), ((), ()))
    scores = [lax.dot_general(q, ref[0], dims, preferred_element_type=jnp.float32) for ref in halves]
    own = jnp.maximum(scores[0].max(axis=1, keepdims=True), scores[1].max(axis=1, keepdims=True))
    top, less = top(own)
    expos = [jnp.exp2((s - less) * const) for s in scores]
    total = expos[0].sum(axis=1, keepdims=True) + expos[1].sum(axis=1, keepdims=True)
    heard = sum(
        jnp.dot(e.astype(jnp.bfloat16), ref[1], preferred_element_type=jnp.float32)
        for e, ref in zip(expos, halves)
    )
    return top, total, heard


def diagonal():
    return lax.broadcasted_iota(jnp.int32, (HD, HD), 0) == lax.broadcasted_iota(jnp.int32, (HD, HD), 1)


def own_block(mask_ref, level_ref, gate_ref, q_ref, kv_ref, m_out, l_out, a_out, aux_out):
    span_at = lax.axis_index(SPAN)
    for distance in (1, 2):
        column = span_at - distance
        usable = jnp.logical_and(column >= 0, mask_ref[span_at, jnp.maximum(column, 0)] > 0)
        value = jnp.where(usable, 1.0, 0.0).astype(jnp.float32)
        aux_out[pl.ds((distance - 1) * 8, 8), :] = jnp.full((8, HD), value, jnp.float32)
    head = lax.axis_index(CHIPS)
    mine = gate_ref[:, pl.ds(pl.multiple_of(head * HD, HD), HD)]
    chosen = lax.broadcasted_iota(jnp.int32, mine.shape, 0) == level_ref[span_at]
    gate = jnp.where(chosen, mine, 0.0).sum(axis=0, keepdims=True)
    aux_out[pl.ds(16, 8), :] = jnp.broadcast_to(gate, (8, HD))
    for t in range(q_ref.shape[0] // TILE):
        at = pl.ds(t * TILE, TILE)
        top, total, heard = weigh(q_ref[at, :], (kv_ref.at[0], kv_ref.at[1]), lambda own: (own, own), CONST)
        m_out[at, :] = jnp.broadcast_to(top, (TILE, HD))
        l_out[at, :] = jnp.broadcast_to(total, (TILE, HD))
        a_out[at, :] = heard


def served_block(q_ref, kv_ref, out_ref):
    rows = q_ref.shape[0]
    eye = diagonal()
    stats = []
    for t in range(rows // TILE):
        at = pl.ds(t * TILE, TILE)
        top, total, heard = weigh(q_ref[at, :], (kv_ref.at[0], kv_ref.at[1]), lambda own: (own, own), CONST)
        out_ref[at, :] = (heard / total).astype(jnp.bfloat16)
        level = top + jnp.log2(total) * (1.0 / CONST)
        for j in range(TILE // HD):
            stats.append(jnp.where(eye, level[j * HD : (j + 1) * HD], 0.0).sum(axis=0, keepdims=True))
    spare = 8 - len(stats)
    level = jnp.concatenate(stats + [jnp.zeros((spare, HD), jnp.float32)], axis=0)
    high = level.astype(jnp.bfloat16).astype(jnp.float32)
    middle = (level - high).astype(jnp.bfloat16).astype(jnp.float32)
    low = level - high - middle
    pieces = jnp.concatenate((high, middle, low, jnp.zeros((8, HD), jnp.float32)), axis=0)
    out_ref[pl.ds(rows, 32), :] = pieces.astype(jnp.bfloat16)


def last_block(aux_ref, q_ref, kv_ref, m_in, l_in, a_in, part_ref, out_ref):
    rows = q_ref.shape[0]
    opened1 = aux_ref[0:1, :1] > 0.5
    opened2 = aux_ref[8:9, :1] > 0.5
    gate = aux_ref[16:17, :]
    eye = diagonal()
    pieces = part_ref[pl.ds(rows, 32), :].astype(jnp.float32)
    level = pieces[0:8] + pieces[8:16] + pieces[16:24]
    for t in range(rows // TILE):
        at = pl.ds(t * TILE, TILE)
        before = m_in[at, :1]
        served = jnp.concatenate(
            [
                jnp.where(eye, level[j : j + 1], 0.0).sum(axis=1, keepdims=True)
                for j in range(t * TILE // HD, (t + 1) * TILE // HD)
            ],
            axis=0,
        )
        known = jnp.where(opened2, jnp.maximum(before, served), before)

        def joined(own):
            top = jnp.where(opened1, jnp.maximum(own, known), known)
            return top, jnp.where(opened1, top, 1e30)

        top, total, heard = weigh(q_ref[at, :], (kv_ref.at[0], kv_ref.at[1]), joined, CONST)
        shrink = jnp.exp2((before - top) * CONST)
        share = jnp.where(opened2, jnp.exp2((jnp.where(opened2, served, top) - top) * CONST), 0.0)
        total = total + l_in[at, :1] * shrink + share
        heard = heard + a_in[at, :] * shrink + part_ref[at, :].astype(jnp.float32) * share
        out_ref[at, :] = (heard / total * gate).astype(jnp.bfloat16)


def call(kernel, out_shape, scalars, *arrays):
    vmem = pl.BlockSpec(memory_space=pltpu.VMEM)
    smem = pl.BlockSpec(memory_space=pltpu.SMEM)
    return pl.pallas_call(
        kernel,
        out_shape=out_shape,
        in_specs=[smem] * len(scalars) + [vmem] * len(arrays),
        out_specs=[vmem] * len(out_shape),
        compiler_params=pltpu.CompilerParams(vmem_limit_bytes=VMEM_LIMIT),
        cost_estimate=pl.CostEstimate(flops=1024, bytes_accessed=1024, transcendentals=0),
    )(*scalars, *arrays)


def on_device(queries, key_rows, value_rows, block_mask, noise_level, gate_table):
    local = queries.shape[1]
    heads = queries.shape[2] // HD
    spans = lax.axis_size(SPAN)
    rows = heads * local

    def exchange(block):
        return lax.all_to_all(block, CHIPS, split_axis=0, concat_axis=0, tiled=True)

    def moved(block, distance):
        route = [(i, i + distance) for i in range(spans) if 0 <= i + distance < spans]
        return lax.ppermute(block, SPAN, route)

    def other_core(block):
        return lax.ppermute(block, "core", [(0, 1), (1, 0)])

    def both_cores(block):
        return lax.all_gather(block, "core")

    mixed = jnp.concatenate((queries[0], key_rows[0], value_rows[0]), axis=0)
    mixed = mixed.reshape(3 * local, heads, HD).transpose(1, 0, 2)
    got = exchange(mixed)
    q = got[:, :local].reshape(rows, HD)
    kv = got[:, local:].reshape(heads, 2, local, HD).transpose(1, 0, 2, 3).reshape(2, rows, HD)

    stat = jax.ShapeDtypeStruct((rows, HD), jnp.float32)
    aux = jax.ShapeDtypeStruct((24, HD), jnp.float32)
    part = jax.ShapeDtypeStruct((rows + 32, HD), jnp.bfloat16)
    kv1 = moved(kv, 1)
    later_q = moved(q, -2)
    kv0 = both_cores(kv)
    *state, aux = call(own_block, [stat, stat, stat, aux], (block_mask, noise_level), gate_table, q, kv0)
    later_q, *state = lax.optimization_barrier((later_q, *state))
    (served,) = call(served_block, [part], (), later_q, kv0)
    part2 = moved(served, 2)
    kv1 = both_cores(kv1)
    (out,) = call(
        last_block, [jax.ShapeDtypeStruct((rows, HD), jnp.bfloat16)], (), aux, q, kv1, *state, part2
    )

    back = exchange(out.reshape(heads, local, HD))
    return back.transpose(1, 0, 2).reshape(1, local, heads * HD)


def solution(mesh):
    parts = Mesh(mesh.devices.reshape(4, 2, 4, 8, 2), ("x", "y_hi", "y_lo", "z", "core"))
    tokens = P(SPAN, CHIPS + ("core",), None)
    return jax.shard_map(
        on_device,
        mesh=parts,
        in_specs=(tokens, tokens, tokens, P(), P(), P()),
        out_specs=tokens,
        check_vma=False,
    )
```

time: 97.5 us -> 83.8 us (0.86); the launches traced: 95.6 us -> 83.5 us
  waiting for transfers between devices: 10.9 us -> 5.33 us
  local copies, waits for them, and re-layouts: 6.55 us -> 2.21 us
  blocking collectives: 54.3 us -> 58.5 us
  between operations: 4.02 us -> 0.18 us
  starting transfers between devices: 12.6 us -> 9.24 us
    ppermute x5 -> x3, waiting for transfers between devices: 10.9 us -> 5.33 us  [moved(): return lax.ppermute(block, SPAN, route)]
    all_gather x0 -> x2, blocking collectives: none -> 4.74 us  [both_cores(): return lax.all_gather(block, 'core')]
    ppermute x5 -> x3, starting transfers between devices: 12.6 us -> 9.24 us  [moved(): return lax.ppermute(block, SPAN, route)]
    dynamic_slice x3 -> x0, local copies, waits for them, and re-layouts: 2.83 us -> none  [the longest x1 1.46 us: allowed(): block_mask[span_at, jnp.maximum(column, 0)] > 0]
    unnamed x9 -> x13, local copies, waits for them, and re-layouts: 2.61 us -> 1.09 us
  transfers between devices with their start and end apart: 5 -> 3, of which waited for: 1 -> 1; matrix products, arithmetic and copies ran while one was open for 3% -> 0% of each run, Pallas kernels for 5% -> 6%
where the time goes in v2:
time: 83.8 us; the launch traced here: 83.5 us
  blocking collectives  58.5 us (70%)
  starting transfers between devices  9.24 us (11%)
  Pallas kernels  8.02 us (10%)
  waiting for transfers between devices  5.33 us (6%)
  local copies, waits for them, and re-layouts  2.21 us (3%)
    all_to_all x2, blocking collectives, exchange(): return lax.all_to_all(block, CHIPS, split_axis=0, concat_axis=0, tiled=True)  53.7 us
    ppermute x3, starting transfers between devices, moved(): return lax.ppermute(block, SPAN, route)  9.24 us
    pallas_call x3, Pallas kernels, call(): pl.pallas_call(kernel, out_shape=out_shape, in_specs=[smem] * len(scalars...  8.02 us
    ppermute x3, waiting for transfers between devices, moved(): return lax.ppermute(block, SPAN, route)  5.33 us
    all_gather x2, blocking collectives, both_cores(): return lax.all_gather(block, 'core')  4.74 us
  transfers between devices with their start and end apart: 3, of which 1 were waited for; matrix products, arithmetic and copies ran while one was open for 0% of the time, Pallas kernels for 6%

profile of v2, /device:TPU:6, one launch (start us, length us, event | category | flops | bytes accessed | tf_op | source)
XLA Modules:
  0.0 83.5 jit_solution(4726068683630627303)
XLA Ops:
  0.0 0.0 copy-start.3
  0.0 0.0 copy-start.4
  0.0 1.0 %copy.17 = bf16[3,8,32,128]{3,2,1,0:T(8,128)(2,1)S(1)} copy(bf16[3,8,32,128]{3,1,2,0:T(8,128)(2,1)} %bitcast.33) | data formatting | bytes 393216
  1.0 0.1 copy.12
  1.1 0.0 copy-done.3
  1.1 0.1 copy.13
  1.2 0.0 copy-done.4
  1.3 0.1 copy.14
  1.4 0.1 maximum_bitcast_fusion
  1.4 31.5 %all_to_all.10 = bf16[32,72,128]{2,1,0:T(8,128)(2,1)S(1)} all-to-all(bf16[32,72,128]{2,1,0:T(8,128)(2,1)S(1)} %maximum_bitcast_fusion), channel_id=1, replica_groups=mesh['x'=4,'y_hi'=2,'y_lo'=4,'z'=8,'core'=2] {'y_lo','z'}, dimensions={0} | all-to-all | bytes 1179648 | tf_op jit(solution)/shard_map/all_to_all | solution.py:129
  33.0 0.0 copy-start
  33.0 0.0 copy-start.1
  33.0 0.0 copy-start.2
  33.1 5.2 %collective-permute-start = (bf16[2,768,128]{2,1,0:T(8,128)(2,1)S(1)}, bf16[2,768,128]{2,1,0:T(8,128)(2,1)S(1)}, u32[]{:S(2)}, u32[]{:S(2)}) collective-permute-start(bf16[2,768,128]{2,1,0:T(8,128)(2,1)S(1)} %bitcast.27), channel_id=1, source_target_pairs={{0,64},{64,128},{128,192},{192,256},{256,320},{320,384},{384,448},... | collective-permute-start | bytes 1179656 | tf_op jit(solution)/shard_map/ppermute | solution.py:133
  38.3 2.7 %collective-permute-start.1 = (bf16[768,128]{1,0:T(8,128)(2,1)S(1)}, bf16[768,128]{1,0:T(8,128)(2,1)S(1)}, u32[]{:S(2)}, u32[]{:S(2)}) collective-permute-start(bf16[768,128]{1,0:T(8,128)(2,1)S(1)} %bitcast.22), channel_id=1, source_target_pairs={{128,0},{192,64},{256,128},{320,192},{384,256},{448,320},{129,1},{... | collective-permute-start | bytes 589832 | tf_op jit(solution)/shard_map/ppermute | solution.py:133
  41.1 2.4 %all_gather.9.kv_ref = bf16[2,2,768,128]{3,2,1,0:T(8,128)(2,1)S(1)} all-gather(bf16[1,2,768,128]{3,2,1,0:T(8,128)(2,1)S(1)} %bitcast.28), channel_id=1, replica_groups=mesh['x'=4,'y_hi'=2,'y_lo'=4,'z'=8,'core'=2] {'core'}, dimensions={0}, use_global_device_ids=true | all-gather | bytes 1179648 | tf_op jit(solution)/shard_map/all_gather | solution.py:139
  43.4 0.0 copy-done
  43.4 0.0 copy-done.1
  43.4 0.0 copy-done.2
  43.4 3.0 %shard_map.64 = (f32[768,128]{1,0:T(8,128)S(1)}, f32[768,128]{1,0:T(8,128)S(1)}, f32[768,128]{1,0:T(8,128)S(1)}, f32[24,128]{1,0:T(8,128)S(1)}) custom-call(s32[8,8]{1,0:T(8,128)S(1)} %copy-done.1, s32[8]{0:T(128)S(1)} %copy-done.2, f32[8,4096]{1,0:T(8,128)S(1)} %copy-done, bf16[768,128]{1,0:T(8,128)(2,1)S(1)} %bitcast.23, ...), custom_call_target="tpu_custom_call" | custom-call | flops 1024 | bytes 1024 | tf_op jit(solution)/shard_map/pallas_call | solution.py:112
  46.4 0.0 collective-permute-done.1.q_ref
  46.4 2.4 %shard_map.65 = bf16[800,128]{1,0:T(8,128)(2,1)S(1)} custom-call(bf16[768,128]{1,0:T(8,128)(2,1)S(1)} %collective-permute-done.1.q_ref, bf16[2,2,768,128]{3,2,1,0:T(8,128)(2,1)S(1)} %all_gather.9.kv_ref), custom_call_target="tpu_custom_call" | custom-call | flops 1024 | bytes 1024 | tf_op jit(solution)/shard_map/pallas_call | solution.py:112
  48.9 1.3 %collective-permute-start.2 = (bf16[800,128]{1,0:T(8,128)(2,1)S(1)}, bf16[800,128]{1,0:T(8,128)(2,1)S(1)}, u32[]{:S(2)}, u32[]{:S(2)}) collective-permute-start(bf16[800,128]{1,0:T(8,128)(2,1)S(1)} %shard_map.65), channel_id=1, source_target_pairs={{0,128},{64,192},{128,256},{192,320},{256,384},{320,448},{1,129},{... | collective-permute-start | bytes 614408 | tf_op jit(solution)/shard_map/ppermute | solution.py:133
  50.2 0.0 collective-permute-done
  50.2 2.4 %all-gather = bf16[4,768,128]{2,1,0:T(8,128)(2,1)S(1)} all-gather(bf16[2,768,128]{2,1,0:T(8,128)(2,1)S(1)} %collective-permute-done), channel_id=2, replica_groups=mesh['x'=4,'y_hi'=2,'y_lo'=4,'z'=8,'core'=2] {'core'}, dimensions={0}, use_global_device_ids=true | all-gather | bytes 1179648 | tf_op jit(solution)/shard_map/all_gather | solution.py:139
  52.5 5.3 %collective-permute-done.2.part_ref = bf16[800,128]{1,0:T(8,128)(2,1)S(1)} collective-permute-done((bf16[800,128]{1,0:T(8,128)(2,1)S(1)}, bf16[800,128]{1,0:T(8,128)(2,1)S(1)}, u32[]{:S(2)}, u32[]{:S(2)}) %collective-permute-start.2) | collective-permute-done | bytes 204832 | tf_op jit(solution)/shard_map/ppermute | solution.py:133
  57.9 2.6 %shard_map.66 = bf16[768,128]{1,0:T(8,128)(2,1)S(1)} custom-call(f32[24,128]{1,0:T(8,128)S(1)} %get-tuple-element.13.aux_ref, bf16[768,128]{1,0:T(8,128)(2,1)S(1)} %bitcast.24, bf16[2,2,768,128]{3,2,1,0:T(8,128)(2,1)S(1)} %bitcast.21, f32[768,128]{1,0:T(8,128)S(1)} %get-tuple-element.17.m_in, f32[768,128]{1,0:T(8,128)S(1)} %get-tuple-element.18.l_in, ...), custom_call_target="tpu_custom_call" | custom-call | flops 1024 | bytes 1024 | tf_op jit(solution)/shard_map/pallas_call | solution.py:112
  60.5 22.2 %all_to_all.11 = bf16[32,24,128]{2,1,0:T(8,128)(2,1)S(1)} all-to-all(bf16[32,24,128]{2,1,0:T(8,128)(2,1)S(1)} %bitcast.25), channel_id=1, replica_groups=mesh['x'=4,'y_hi'=2,'y_lo'=4,'z'=8,'core'=2] {'y_lo','z'}, dimensions={0} | all-to-all | bytes 393216 | tf_op jit(solution)/shard_map/all_to_all | solution.py:129
  82.8 0.8 reshape.26
  (6 shorter events, 0.2 us)
Async XLA Ops:
  0.0 1.1 %copy-start.3 = (bf16[1,24,4096]{2,1,0:T(8,128)(2,1)S(1)}, bf16[1,24,4096]{2,1,0:T(8,128)(2,1)}, u32[]{:S(2)}) copy-start(bf16[1,24,4096]{2,1,0:T(8,128)(2,1)} %param.7) | copy-start | bytes 589828
  0.0 1.2 %copy-start.4 = (bf16[1,24,4096]{2,1,0:T(8,128)(2,1)S(1)}, bf16[1,24,4096]{2,1,0:T(8,128)(2,1)}, u32[]{:S(2)}) copy-start(bf16[1,24,4096]{2,1,0:T(8,128)(2,1)} %param.8) | copy-start | bytes 589828
  33.0 10.4 %copy-start = (f32[8,4096]{1,0:T(8,128)S(1)}, f32[8,4096]{1,0:T(8,128)}, u32[]{:S(2)}) copy-start(f32[8,4096]{1,0:T(8,128)} %gate_ref.1) | copy-start | bytes 393220
  33.0 10.4 %copy-start.1 = (s32[8,8]{1,0:T(8,128)S(1)}, s32[8,8]{1,0:T(8,128)}, u32[]{:S(2)}) copy-start(s32[8,8]{1,0:T(8,128)} %mask_ref.1) | copy-start | bytes 772
  33.0 10.4 %copy-start.2 = (s32[8]{0:T(128)S(1)}, s32[8]{0:T(128)}, u32[]{:S(2)}) copy-start(s32[8]{0:T(128)} %level_ref.1) | copy-start | bytes 100
  33.1 17.1 %collective-permute-start = (bf16[2,768,128]{2,1,0:T(8,128)(2,1)S(1)}, bf16[2,768,128]{2,1,0:T(8,128)(2,1)S(1)}, u32[]{:S(2)}, u32[]{:S(2)}) collective-permute-start(bf16[2,768,128]{2,1,0:T(8,128)(2,1)S(1)} %bitcast.27), channel_id=1, source_target_pairs={{0,64},{64,128},{128,192},{192,256},{256,320},{320,384},{384,448},... | collective-permute-start | bytes 1179656 | tf_op jit(solution)/shard_map/ppermute | solution.py:133
  38.3 8.1 %collective-permute-start.1 = (bf16[768,128]{1,0:T(8,128)(2,1)S(1)}, bf16[768,128]{1,0:T(8,128)(2,1)S(1)}, u32[]{:S(2)}, u32[]{:S(2)}) collective-permute-start(bf16[768,128]{1,0:T(8,128)(2,1)S(1)} %bitcast.22), channel_id=1, source_target_pairs={{128,0},{192,64},{256,128},{320,192},{384,256},{448,320},{129,1},{... | collective-permute-start | bytes 589832 | tf_op jit(solution)/shard_map/ppermute | solution.py:133
  48.9 9.0 %collective-permute-start.2 = (bf16[800,128]{1,0:T(8,128)(2,1)S(1)}, bf16[800,128]{1,0:T(8,128)(2,1)S(1)}, u32[]{:S(2)}, u32[]{:S(2)}) collective-permute-start(bf16[800,128]{1,0:T(8,128)(2,1)S(1)} %shard_map.65), channel_id=1, source_target_pairs={{0,128},{64,192},{128,256},{192,320},{256,384},{320,448},{1,129},{... | collective-permute-start | bytes 614408 | tf_op jit(solution)/shard_map/ppermute | solution.py:133

commit v3 on v2

--- a/solution.py
+++ b/solution.py
@@ -1,7 +1,8 @@
-import functools
+import math
 
 import jax
 import jax.numpy as jnp
+import numpy as np
 from jax import lax
 from jax.experimental import pallas as pl
 from jax.experimental.pallas import tpu as pltpu
@@ -11,9 +12,10 @@
 HD = 128
 SPAN = ("x", "y_hi")
 CHIPS = ("y_lo", "z")
+AXES = SPAN + CHIPS + ("core",)
 CONST = HD ** (-0.5) * 1.4426950408889634
 TILE = 384
-VMEM_LIMIT = 48 * 1024 * 1024
+VMEM_LIMIT = 24 * 1024 * 1024
 
 
 def weigh(q, halves, top, const):
@@ -41,7 +43,10 @@
         usable = jnp.logical_and(column >= 0, mask_ref[span_at, jnp.maximum(column, 0)] > 0)
         value = jnp.where(usable, 1.0, 0.0).astype(jnp.float32)
         aux_out[pl.ds((distance - 1) * 8, 8), :] = jnp.full((8, HD), value, jnp.float32)
-    head = lax.axis_index(CHIPS)
+    line, depth = lax.axis_size("y_lo"), lax.axis_size("z")
+    at_line = lax.axis_index("y_lo")
+    at_line = jnp.where(lax.axis_index("y_hi") > 0, line - 1 - at_line, at_line)
+    head = at_line * depth + lax.axis_index("z")
     mine = gate_ref[:, pl.ds(pl.multiple_of(head * HD, HD), HD)]
     chosen = lax.broadcasted_iota(jnp.int32, mine.shape, 0) == level_ref[span_at]
     gate = jnp.where(chosen, mine, 0.0).sum(axis=0, keepdims=True)
@@ -74,36 +79,55 @@
     out_ref[pl.ds(rows, 32), :] = pieces.astype(jnp.bfloat16)
 
 
-def last_block(aux_ref, q_ref, kv_ref, m_in, l_in, a_in, part_ref, out_ref):
-    rows = q_ref.shape[0]
-    opened1 = aux_ref[0:1, :1] > 0.5
-    opened2 = aux_ref[8:9, :1] > 0.5
+def earlier_block(aux_ref, q_ref, kv_ref, m_in, l_in, a_in, m_out, l_out, a_out):
+    opened = aux_ref[0:1, :1] > 0.5
+    for t in range(q_ref.shape[0] // TILE):
+        at = pl.ds(t * TILE, TILE)
+        before = m_in[at, :1]
+
+        def joined(own):
+            top = jnp.where(opened, jnp.maximum(own, before), before)
+            return top, jnp.where(opened, top, 1e30)
+
+        top, total, heard = weigh(q_ref[at, :], (kv_ref.at[0], kv_ref.at[1]), joined, CONST)
+        shrink = jnp.exp2((before - top) * CONST)
+        m_out[at, :] = jnp.broadcast_to(top, (TILE, HD))
+        l_out[at, :] = jnp.broadcast_to(total + l_in[at, :1] * shrink, (TILE, HD))
+        a_out[at, :] = heard + a_in[at, :] * shrink
+
+
+def join(aux_ref, m_in, l_in, a_in, part_ref, out_ref):
+    rows = m_in.shape[0]
+    opened = aux_ref[8:9, :1] > 0.5
     gate = aux_ref[16:17, :]
     eye = diagonal()
     pieces = part_ref[pl.ds(rows, 32), :].astype(jnp.float32)
     level = pieces[0:8] + pieces[8:16] + pieces[16:24]
-    for t in range(rows // TILE):
-        at = pl.ds(t * TILE, TILE)
-        before = m_in[at, :1]
-        served = jnp.concatenate(
-            [
-                jnp.where(eye, level[j : j + 1], 0.0).sum(axis=1, keepdims=True)
-                for j in range(t * TILE // HD, (t + 1) * TILE // HD)
-            ],
-            axis=0,
-        )
-        known = jnp.where(opened2, jnp.maximum(before, served), before)
-
-        def joined(own):
-            top = jnp.where(opened1, jnp.maximum(own, known), known)
-            return top, jnp.where(opened1, top, 1e30)
-
-        top, total, heard = weigh(q_ref[at, :], (kv_ref.at[0], kv_ref.at[1]), joined, CONST)
+    for t in range(rows // HD):
+        at = pl.ds(t * HD, HD)
+        before = m_in[at, :]
+        served = jnp.where(eye, level[t : t + 1], 0.0).sum(axis=1, keepdims=True)
+        served = jnp.where(opened, served, before)
+        top = jnp.maximum(before, served)
         shrink = jnp.exp2((before - top) * CONST)
-        share = jnp.where(opened2, jnp.exp2((jnp.where(opened2, served, top) - top) * CONST), 0.0)
-        total = total + l_in[at, :1] * shrink + share
-        heard = heard + a_in[at, :] * shrink + part_ref[at, :].astype(jnp.float32) * share
+        share = jnp.where(opened, jnp.exp2((served - top) * CONST), 0.0)
+        total = l_in[at, :] * shrink + share
+        heard = a_in[at, :] * shrink + part_ref[at, :].astype(jnp.float32) * share
         out_ref[at, :] = (heard / total * gate).astype(jnp.bfloat16)
+
+
+def split_heads(q_hbm, k_hbm, v_hbm, out_ref, *held_and_sems):
+    held, sems = held_and_sems[:3], held_and_sems[3:]
+    copies = [
+        pltpu.make_async_copy(source, target, sem)
+        for source, target, sem in zip((q_hbm, k_hbm, v_hbm), held, sems)
+    ]
+    for copy in copies:
+        copy.start()
+    for i, (copy, ref) in enumerate(zip(copies, held)):
+        copy.wait()
+        for h in range(out_ref.shape[0]):
+            out_ref[h, i] = ref[0, :, h * HD : (h + 1) * HD]
 
 
 def call(kernel, out_shape, scalars, *arrays):
@@ -125,8 +149,23 @@
     spans = lax.axis_size(SPAN)
     rows = heads * local
 
+    sizes = [lax.axis_size(axis) for axis in AXES]
+    line = sizes[2]
+    number = np.arange(math.prod(sizes)).reshape(sizes)
+    number[:, 1] = number[:, 1, ::-1].copy()
+    groups = number.transpose(0, 1, 4, 2, 3).reshape(-1, heads).tolist()
+
+    def to_next(block):
+        route = []
+        for at, index in enumerate(np.ndindex(spans, line)):
+            if index[0] + 1 < spans:
+                route.append((at, (index[0] + 1) * line + line - 1 - index[1]))
+        return lax.ppermute(block, SPAN + ("y_lo",), route)
+
     def exchange(block):
-        return lax.all_to_all(block, CHIPS, split_axis=0, concat_axis=0, tiled=True)
+        return lax.all_to_all(
+            block, AXES, split_axis=0, concat_axis=0, axis_index_groups=groups, tiled=True
+        )
 
     def moved(block, distance):
         route = [(i, i + distance) for i in range(spans) if 0 <= i + distance < spans]
@@ -138,16 +177,23 @@
     def both_cores(block):
         return lax.all_gather(block, "core")
 
-    mixed = jnp.concatenate((queries[0], key_rows[0], value_rows[0]), axis=0)
-    mixed = mixed.reshape(3 * local, heads, HD).transpose(1, 0, 2)
+    by_head = jax.ShapeDtypeStruct((heads, 3, local, HD), queries.dtype)
+    mixed = pl.pallas_call(
+        split_heads,
+        out_shape=by_head,
+        in_specs=[pl.BlockSpec(memory_space=pltpu.HBM)] * 3,
+        out_specs=pl.BlockSpec(memory_space=pltpu.VMEM),
+        scratch_shapes=[pltpu.VMEM(queries.shape, queries.dtype)] * 3 + [pltpu.SemaphoreType.DMA] * 3,
+        compiler_params=pltpu.CompilerParams(vmem_limit_bytes=VMEM_LIMIT),
+    )(queries, key_rows, value_rows)
     got = exchange(mixed)
-    q = got[:, :local].reshape(rows, HD)
-    kv = got[:, local:].reshape(heads, 2, local, HD).transpose(1, 0, 2, 3).reshape(2, rows, HD)
+    q = got[:, 0].reshape(rows, HD)
+    kv = got[:, 1:].transpose(1, 0, 2, 3).reshape(2, rows, HD)
 
     stat = jax.ShapeDtypeStruct((rows, HD), jnp.float32)
     aux = jax.ShapeDtypeStruct((24, HD), jnp.float32)
     part = jax.ShapeDtypeStruct((rows + 32, HD), jnp.bfloat16)
-    kv1 = moved(kv, 1)
+    kv1 = to_next(kv)
     later_q = moved(q, -2)
     kv0 = both_cores(kv)
     *state, aux = call(own_block, [stat, stat, stat, aux], (block_mask, noise_level), gate_table, q, kv0)
@@ -155,9 +201,8 @@
     (served,) = call(served_block, [part], (), later_q, kv0)
     part2 = moved(served, 2)
     kv1 = both_cores(kv1)
-    (out,) = call(
-        last_block, [jax.ShapeDtypeStruct((rows, HD), jnp.bfloat16)], (), aux, q, kv1, *state, part2
-    )
+    state = call(earlier_block, [stat, stat, stat], (), aux, q, kv1, *state)
+    (out,) = call(join, [jax.ShapeDtypeStruct((rows, HD), jnp.bfloat16)], (), aux, *state, part2)
 
     back = exchange(out.reshape(heads, local, HD))
     return back.transpose(1, 0, 2).reshape(1, local, heads * HD)

time: 83.8 us -> 81.8 us (0.976)
  blocking collectives: 58.5 us -> 55.1 us
  local copies, waits for them, and re-layouts: 2.21 us -> 3.69 us
  Pallas kernels: 8.02 us -> 9.24 us
    ppermute x3 -> x2, waiting for transfers between devices: 5.33 us -> 0.01 us  [moved(): return lax.ppermute(block, SPAN, route)]
    ppermute x3 -> x2, starting transfers between devices: 9.24 us -> 4.04 us  [moved(): return lax.ppermute(block, SPAN, route)]
    ppermute x0 -> x1, starting transfers between devices: none -> 4.7 us  [to_next(): return lax.ppermute(block, SPAN + ('y_lo',), route)]
    ppermute x0 -> x1, waiting for transfers between devices: none -> 4.55 us  [to_next(): return lax.ppermute(block, SPAN + ('y_lo',), route)]
    all_to_all x2, blocking collectives: 53.7 us -> 50.3 us  [exchange(): lax.all_to_all(block, AXES, split_axis=0, concat_axis=0, axis_index_group...]
    unnamed x13 -> x12, local copies, waits for them, and re-layouts: 1.09 us -> 2.8 us
    pallas_call x0 -> x1, Pallas kernels: none -> 0.85 us  [on_device(): pl.pallas_call(split_heads, out_shape=by_head, in_specs=[pl.BlockSpec(mem...]
    pallas_call x3 -> x4, Pallas kernels: 8.02 us -> 8.38 us  [call(): pl.pallas_call(kernel, out_shape=out_shape, in_specs=[smem] * len(scalars...]
  transfers between devices with their start and end apart: 3 -> 3, of which waited for: 1 -> 1; matrix products, arithmetic and copies ran while one was open for 0% -> 0% of each run, Pallas kernels for 6% -> 10%
where the time goes in v3:
time: 81.8 us; the launch traced here: 81.5 us
  blocking collectives  55.1 us (67%)
  Pallas kernels  9.24 us (11%)
  starting transfers between devices  8.73 us (11%)
  waiting for transfers between devices  4.56 us (6%)
  local copies, waits for them, and re-layouts  3.69 us (5%)
    all_to_all x2, blocking collectives, exchange(): lax.all_to_all(block, AXES, split_axis=0, concat_axis=0, axis_index_group...  50.3 us
    pallas_call x4, Pallas kernels, call(): pl.pallas_call(kernel, out_shape=out_shape, in_specs=[smem] * len(scalars...  8.38 us
    all_gather x2, blocking collectives, both_cores(): return lax.all_gather(block, 'core')  4.86 us
    ppermute x1, starting transfers between devices, to_next(): return lax.ppermute(block, SPAN + ('y_lo',), route)  4.7 us
    ppermute x1, waiting for transfers between devices, to_next(): return lax.ppermute(block, SPAN + ('y_lo',), route)  4.55 us
    ppermute x2, starting transfers between devices, moved(): return lax.ppermute(block, SPAN, route)  4.04 us
    unnamed x12, local copies, waits for them, and re-layouts  2.8 us
  transfers between devices with their start and end apart: 3, of which 1 were waited for; matrix products, arithmetic and copies ran while one was open for 0% of the time, Pallas kernels for 10%

profile of v3, /device:TPU:6, one launch (start us, length us, event | category | flops | bytes accessed | tf_op | source)
XLA Modules:
  0.0 81.5 jit_solution(6806939481251313647)
XLA Ops:
  0.0 0.0 copy-start
  0.0 0.9 %copy-done = bf16[1,24,4096]{2,1,0:T(8,128)(2,1)S(1)} copy-done((bf16[1,24,4096]{2,1,0:T(8,128)(2,1)S(1)}, bf16[1,24,4096]{2,1,0:T(8,128)(2,1)}, u32[]{:S(2)}) %copy-start) | copy-done | bytes 196632
  0.9 0.0 copy-start.1
  0.9 0.9 %copy-done.1 = bf16[1,24,4096]{2,1,0:T(8,128)(2,1)S(1)} copy-done((bf16[1,24,4096]{2,1,0:T(8,128)(2,1)S(1)}, bf16[1,24,4096]{2,1,0:T(8,128)(2,1)}, u32[]{:S(2)}) %copy-start.1) | copy-done | bytes 196632
  1.9 0.0 copy-start.2
  1.9 0.9 %copy-done.2 = bf16[1,24,4096]{2,1,0:T(8,128)(2,1)S(1)} copy-done((bf16[1,24,4096]{2,1,0:T(8,128)(2,1)S(1)}, bf16[1,24,4096]{2,1,0:T(8,128)(2,1)}, u32[]{:S(2)}) %copy-start.2) | copy-done | bytes 196632
  2.8 0.9 %shard_map.64 = bf16[32,3,24,128]{3,2,1,0:T(8,128)(2,1)S(1)} custom-call(bf16[1,24,4096]{2,1,0:T(8,128)(2,1)S(1)} %copy-done, bf16[1,24,4096]{2,1,0:T(8,128)(2,1)S(1)} %copy-done.1, bf16[1,24,4096]{2,1,0:T(8,128)(2,1)S(1)} %copy-done.2), custom_call_target="tpu_custom_call" | custom-call | tf_op jit(solution)/shard_map/pallas_call | solution.py:181
  3.6 31.5 %all_to_all.10 = bf16[32,3,24,128]{3,2,1,0:T(8,128)(2,1)S(1)} all-to-all(bf16[32,3,24,128]{3,2,1,0:T(8,128)(2,1)S(1)} %shard_map.64), channel_id=1, replica_groups={{0,2,4,6,8,10,12,14,16,18,20,22,24,26,28,30,32,34,36,38,40,42,44,46,48,..., dimensions={0} | all-to-all | bytes 1179648 | tf_op jit(solution)/shard_map/all_to_all | solution.py:166
  35.2 4.7 %collective-permute-start = (bf16[2,768,128]{2,1,0:T(8,128)(2,1)S(1)}, bf16[2,768,128]{2,1,0:T(8,128)(2,1)S(1)}, u32[]{:S(2)}, u32[]{:S(2)}) collective-permute-start(bf16[2,768,128]{2,1,0:T(8,128)(2,1)S(1)} %bitcast.13), channel_id=1, source_target_pairs={{0,112},{16,96},{32,80},{48,64},{64,176},{80,160},{96,144},{112,12... | collective-permute-start | bytes 1179656 | tf_op jit(solution)/shard_map/ppermute | solution.py:163
  40.0 2.7 %collective-permute-start.1 = (bf16[768,128]{1,0:T(8,128)(2,1)S(1)}, bf16[768,128]{1,0:T(8,128)(2,1)S(1)}, u32[]{:S(2)}, u32[]{:S(2)}) collective-permute-start(bf16[768,128]{1,0:T(8,128)(2,1)S(1)} %bitcast.9), channel_id=1, source_target_pairs={{128,0},{192,64},{256,128},{320,192},{384,256},{448,320},{129,1},{... | collective-permute-start | bytes 589832 | tf_op jit(solution)/shard_map/ppermute | solution.py:172
  42.7 0.0 copy-start.3
  42.7 0.0 copy-start.4
  42.8 0.0 copy-start.5
  42.8 2.5 %all_gather.9.kv_ref = bf16[2,2,768,128]{3,2,1,0:T(8,128)(2,1)S(1)} all-gather(bf16[1,2,768,128]{3,2,1,0:T(8,128)(2,1)S(1)} %bitcast.14), channel_id=1, replica_groups=mesh['x'=4,'y_hi'=2,'y_lo'=4,'z'=8,'core'=2] {'core'}, dimensions={0}, use_global_device_ids=true | all-gather | bytes 1179648 | tf_op jit(solution)/shard_map/all_gather | solution.py:178
  45.3 0.0 copy-done.3
  45.3 0.0 copy-done.4
  45.3 0.0 copy-done.5
  45.3 3.0 %shard_map.65 = (f32[768,128]{1,0:T(8,128)S(1)}, f32[768,128]{1,0:T(8,128)S(1)}, f32[768,128]{1,0:T(8,128)S(1)}, f32[24,128]{1,0:T(8,128)S(1)}) custom-call(s32[8,8]{1,0:T(8,128)S(1)} %copy-done.4, s32[8]{0:T(128)S(1)} %copy-done.5, f32[8,4096]{1,0:T(8,128)S(1)} %copy-done.3, bf16[768,128]{1,0:T(8,128)(2,1)S(1)} %bitcast.10, ...), custom_call_target="tpu_custom_call" | custom-call | flops 1024 | bytes 1024 | tf_op jit(solution)/shard_map/pallas_call | solution.py:136
  48.3 0.0 collective-permute-done.1.q_ref
  48.3 2.4 %shard_map.67 = bf16[800,128]{1,0:T(8,128)(2,1)S(1)} custom-call(bf16[768,128]{1,0:T(8,128)(2,1)S(1)} %collective-permute-done.1.q_ref, bf16[2,2,768,128]{3,2,1,0:T(8,128)(2,1)S(1)} %all_gather.9.kv_ref), custom_call_target="tpu_custom_call" | custom-call | flops 1024 | bytes 1024 | tf_op jit(solution)/shard_map/pallas_call | solution.py:136
  50.8 1.3 %collective-permute-start.2 = (bf16[800,128]{1,0:T(8,128)(2,1)S(1)}, bf16[800,128]{1,0:T(8,128)(2,1)S(1)}, u32[]{:S(2)}, u32[]{:S(2)}) collective-permute-start(bf16[800,128]{1,0:T(8,128)(2,1)S(1)} %shard_map.67), channel_id=1, source_target_pairs={{0,128},{64,192},{128,256},{192,320},{256,384},{320,448},{1,129},{... | collective-permute-start | bytes 614408 | tf_op jit(solution)/shard_map/ppermute | solution.py:172
  52.1 4.6 %collective-permute-done = bf16[2,768,128]{2,1,0:T(8,128)(2,1)S(1)} collective-permute-done((bf16[2,768,128]{2,1,0:T(8,128)(2,1)S(1)}, bf16[2,768,128]{2,1,0:T(8,128)(2,1)S(1)}, u32[]{:S(2)}, u32[]{:S(2)}) %collective-permute-start) | collective-permute-done | bytes 393248 | tf_op jit(solution)/shard_map/ppermute | solution.py:163
  56.6 2.4 %all-gather = bf16[4,768,128]{2,1,0:T(8,128)(2,1)S(1)} all-gather(bf16[2,768,128]{2,1,0:T(8,128)(2,1)S(1)} %collective-permute-done), channel_id=2, replica_groups=mesh['x'=4,'y_hi'=2,'y_lo'=4,'z'=8,'core'=2] {'core'}, dimensions={0}, use_global_device_ids=true | all-gather | bytes 1179648 | tf_op jit(solution)/shard_map/all_gather | solution.py:178
  59.0 2.6 %shard_map.66 = (f32[768,128]{1,0:T(8,128)S(1)}, f32[768,128]{1,0:T(8,128)S(1)}, f32[768,128]{1,0:T(8,128)S(1)}) custom-call(f32[24,128]{1,0:T(8,128)S(1)} %get-tuple-element.16.aux_ref, bf16[768,128]{1,0:T(8,128)(2,1)S(1)} %bitcast.11, bf16[2,2,768,128]{3,2,1,0:T(8,128)(2,1)S(1)} %bitcast.8, f32[768,128]{1,0:T(8,128)S(1)} %get-tuple-element.20.m_in, ...), custom_call_target="tpu_custom_call" | custom-call | flops 1024 | bytes 1024 | tf_op jit(solution)/shard_map/pallas_call | solution.py:136
  61.6 0.0 collective-permute-done.2.part_ref
  61.6 0.3 shard_map.68
  61.9 18.8 %all_to_all.11 = bf16[32,24,128]{2,1,0:T(8,128)(2,1)S(1)} all-to-all(bf16[32,24,128]{2,1,0:T(8,128)(2,1)S(1)} %bitcast.12), channel_id=1, replica_groups={{0,2,4,6,8,10,12,14,16,18,20,22,24,26,28,30,32,34,36,38,40,42,44,46,48,..., dimensions={0} | all-to-all | bytes 393216 | tf_op jit(solution)/shard_map/all_to_all | solution.py:166
  80.7 0.8 reshape.11
  (4 shorter events, 0.1 us)
Async XLA Ops:
  0.0 0.9 %copy-start = (bf16[1,24,4096]{2,1,0:T(8,128)(2,1)S(1)}, bf16[1,24,4096]{2,1,0:T(8,128)(2,1)}, u32[]{:S(2)}) copy-start(bf16[1,24,4096]{2,1,0:T(8,128)(2,1)} %q_hbm.1) | copy-start | bytes 589828
  0.9 0.9 %copy-start.1 = (bf16[1,24,4096]{2,1,0:T(8,128)(2,1)S(1)}, bf16[1,24,4096]{2,1,0:T(8,128)(2,1)}, u32[]{:S(2)}) copy-start(bf16[1,24,4096]{2,1,0:T(8,128)(2,1)} %k_hbm.1) | copy-start | bytes 589828
  1.9 0.9 %copy-start.2 = (bf16[1,24,4096]{2,1,0:T(8,128)(2,1)S(1)}, bf16[1,24,4096]{2,1,0:T(8,128)(2,1)}, u32[]{:S(2)}) copy-start(bf16[1,24,4096]{2,1,0:T(8,128)(2,1)} %v_hbm.1) | copy-start | bytes 589828
  35.2 21.4 %collective-permute-start = (bf16[2,768,128]{2,1,0:T(8,128)(2,1)S(1)}, bf16[2,768,128]{2,1,0:T(8,128)(2,1)S(1)}, u32[]{:S(2)}, u32[]{:S(2)}) collective-permute-start(bf16[2,768,128]{2,1,0:T(8,128)(2,1)S(1)} %bitcast.13), channel_id=1, source_target_pairs={{0,112},{16,96},{32,80},{48,64},{64,176},{80,160},{96,144},{112,12... | collective-permute-start | bytes 1179656 | tf_op jit(solution)/shard_map/ppermute | solution.py:163
  40.0 8.3 %collective-permute-start.1 = (bf16[768,128]{1,0:T(8,128)(2,1)S(1)}, bf16[768,128]{1,0:T(8,128)(2,1)S(1)}, u32[]{:S(2)}, u32[]{:S(2)}) collective-permute-start(bf16[768,128]{1,0:T(8,128)(2,1)S(1)} %bitcast.9), channel_id=1, source_target_pairs={{128,0},{192,64},{256,128},{320,192},{384,256},{448,320},{129,1},{... | collective-permute-start | bytes 589832 | tf_op jit(solution)/shard_map/ppermute | solution.py:172
  42.7 2.5 %copy-start.3 = (f32[8,4096]{1,0:T(8,128)S(1)}, f32[8,4096]{1,0:T(8,128)}, u32[]{:S(2)}) copy-start(f32[8,4096]{1,0:T(8,128)} %gate_ref.1) | copy-start | bytes 393220
  42.7 2.5 %copy-start.4 = (s32[8,8]{1,0:T(8,128)S(1)}, s32[8,8]{1,0:T(8,128)}, u32[]{:S(2)}) copy-start(s32[8,8]{1,0:T(8,128)} %mask_ref.1) | copy-start | bytes 772
  42.8 2.5 %copy-start.5 = (s32[8]{0:T(128)S(1)}, s32[8]{0:T(128)}, u32[]{:S(2)}) copy-start(s32[8]{0:T(128)} %level_ref.1) | copy-start | bytes 100
  50.8 10.8 %collective-permute-start.2 = (bf16[800,128]{1,0:T(8,128)(2,1)S(1)}, bf16[800,128]{1,0:T(8,128)(2,1)S(1)}, u32[]{:S(2)}, u32[]{:S(2)}) collective-permute-start(bf16[800,128]{1,0:T(8,128)(2,1)S(1)} %shard_map.67), channel_id=1, source_target_pairs={{0,128},{64,192},{128,256},{192,320},{256,384},{320,448},{1,129},{... | collective-permute-start | bytes 614408 | tf_op jit(solution)/shard_map/ppermute | solution.py:172

commit v4 on v3

--- a/solution.py
+++ b/solution.py
@@ -1,5 +1,3 @@
-import math
-
 import jax
 import jax.numpy as jnp
 import numpy as np
@@ -12,7 +10,6 @@
 HD = 128
 SPAN = ("x", "y_hi")
 CHIPS = ("y_lo", "z")
-AXES = SPAN + CHIPS + ("core",)
 CONST = HD ** (-0.5) * 1.4426950408889634
 TILE = 384
 VMEM_LIMIT = 24 * 1024 * 1024
@@ -43,10 +40,7 @@
         usable = jnp.logical_and(column >= 0, mask_ref[span_at, jnp.maximum(column, 0)] > 0)
         value = jnp.where(usable, 1.0, 0.0).astype(jnp.float32)
         aux_out[pl.ds((distance - 1) * 8, 8), :] = jnp.full((8, HD), value, jnp.float32)
-    line, depth = lax.axis_size("y_lo"), lax.axis_size("z")
-    at_line = lax.axis_index("y_lo")
-    at_line = jnp.where(lax.axis_index("y_hi") > 0, line - 1 - at_line, at_line)
-    head = at_line * depth + lax.axis_index("z")
+    head = placed(lax.axis_index("y_lo") * lax.axis_size("z") + lax.axis_index("z"))
     mine = gate_ref[:, pl.ds(pl.multiple_of(head * HD, HD), HD)]
     chosen = lax.broadcasted_iota(jnp.int32, mine.shape, 0) == level_ref[span_at]
     gate = jnp.where(chosen, mine, 0.0).sum(axis=0, keepdims=True)
@@ -116,6 +110,12 @@
         out_ref[at, :] = (heard / total * gate).astype(jnp.bfloat16)
 
 
+def placed(index):
+    line, depth = lax.axis_size("y_lo"), lax.axis_size("z")
+    at, z = index // depth, index % depth
+    return jnp.where(lax.axis_index("y_hi") > 0, line - 1 - at, at) * depth + z
+
+
 def split_heads(q_hbm, k_hbm, v_hbm, out_ref, *held_and_sems):
     held, sems = held_and_sems[:3], held_and_sems[3:]
     copies = [
@@ -127,7 +127,12 @@
     for i, (copy, ref) in enumerate(zip(copies, held)):
         copy.wait()
         for h in range(out_ref.shape[0]):
-            out_ref[h, i] = ref[0, :, h * HD : (h + 1) * HD]
+            out_ref[placed(h), i] = ref[0, :, h * HD : (h + 1) * HD]
+
+
+def join_heads(in_ref, out_ref):
+    for h in range(in_ref.shape[0]):
+        out_ref[0, :, h * HD : (h + 1) * HD] = in_ref[placed(h)]
 
 
 def call(kernel, out_shape, scalars, *arrays):
@@ -149,11 +154,7 @@
     spans = lax.axis_size(SPAN)
     rows = heads * local
 
-    sizes = [lax.axis_size(axis) for axis in AXES]
-    line = sizes[2]
-    number = np.arange(math.prod(sizes)).reshape(sizes)
-    number[:, 1] = number[:, 1, ::-1].copy()
-    groups = number.transpose(0, 1, 4, 2, 3).reshape(-1, heads).tolist()
+    line = lax.axis_size("y_lo")
 
     def to_next(block):
         route = []
@@ -163,9 +164,7 @@
         return lax.ppermute(block, SPAN + ("y_lo",), route)
 
     def exchange(block):
-        return lax.all_to_all(
-            block, AXES, split_axis=0, concat_axis=0, axis_index_groups=groups, tiled=True
-        )
+        return lax.all_to_all(block, CHIPS, split_axis=0, concat_axis=0, tiled=True)
 
     def moved(block, distance):
         route = [(i, i + distance) for i in range(spans) if 0 <= i + distance < spans]
@@ -184,7 +183,7 @@
         in_specs=[pl.BlockSpec(memory_space=pltpu.HBM)] * 3,
         out_specs=pl.BlockSpec(memory_space=pltpu.VMEM),
         scratch_shapes=[pltpu.VMEM(queries.shape, queries.dtype)] * 3 + [pltpu.SemaphoreType.DMA] * 3,
-        compiler_params=pltpu.CompilerParams(vmem_limit_bytes=VMEM_LIMIT),
+        compiler_params=pltpu.CompilerParams(vmem_limit_bytes=60 * 1024 * 1024),
     )(queries, key_rows, value_rows)
     got = exchange(mixed)
     q = got[:, 0].reshape(rows, HD)
@@ -205,7 +204,8 @@
     (out,) = call(join, [jax.ShapeDtypeStruct((rows, HD), jnp.bfloat16)], (), aux, *state, part2)
 
     back = exchange(out.reshape(heads, local, HD))
-    return back.transpose(1, 0, 2).reshape(1, local, heads * HD)
+    (attended,) = call(join_heads, [jax.ShapeDtypeStruct(queries.shape, queries.dtype)], (), back)
+    return attended
 
 
 def solution(mesh):

time: 81.8 us -> 80.3 us (0.982)
  local copies, waits for them, and re-layouts: 3.69 us -> 0.12 us
  Pallas kernels: 9.24 us -> 11.1 us
  waiting for transfers between devices: 4.56 us -> 5.89 us
    unnamed x12 -> x6, local copies, waits for them, and re-layouts: 2.8 us -> 0.02 us
    ppermute x1, waiting for transfers between devices: 4.55 us -> 5.88 us  [to_next(): return lax.ppermute(block, SPAN + ('y_lo',), route)]
    pallas_call x1, Pallas kernels: 0.85 us -> 1.98 us  [on_device(): pl.pallas_call(split_heads, out_shape=by_head, in_specs=[pl.BlockSpec(mem...]
    pallas_call x4 -> x5, Pallas kernels: 8.38 us -> 9.07 us  [call(): pl.pallas_call(kernel, out_shape=out_shape, in_specs=[smem] * len(scalars...]
where the time goes in v4:
time: 80.3 us; the launch traced here: 79.9 us
  blocking collectives  54.3 us (68%)
  Pallas kernels  11.1 us (14%)
  starting transfers between devices  8.44 us (11%)
  waiting for transfers between devices  5.89 us (7%)
    all_to_all x2, blocking collectives, exchange(): return lax.all_to_all(block, CHIPS, split_axis=0, concat_axis=0, tiled=True)  49.5 us
    pallas_call x5, Pallas kernels, call(): pl.pallas_call(kernel, out_shape=out_shape, in_specs=[smem] * len(scalars...  9.07 us
    ppermute x1, waiting for transfers between devices, to_next(): return lax.ppermute(block, SPAN + ('y_lo',), route)  5.88 us
    all_gather x2, blocking collectives, both_cores(): return lax.all_gather(block, 'core')  4.86 us
    ppermute x1, starting transfers between devices, to_next(): return lax.ppermute(block, SPAN + ('y_lo',), route)  4.4 us
    ppermute x2, starting transfers between devices, moved(): return lax.ppermute(block, SPAN, route)  4.04 us
    pallas_call x1, Pallas kernels, on_device(): pl.pallas_call(split_heads, out_shape=by_head, in_specs=[pl.BlockSpec(mem...  1.98 us
  transfers between devices with their start and end apart: 3, of which 1 were waited for; matrix products, arithmetic and copies ran while one was open for 0% of the time, Pallas kernels for 10%

profile of v4, /device:TPU:6, one launch (start us, length us, event | category | flops | bytes accessed | tf_op | source)
XLA Modules:
  0.0 79.9 jit_solution(11527304647284598958)
XLA Ops:
  0.0 2.0 %shard_map.64 = bf16[32,3,24,128]{3,2,1,0:T(8,128)(2,1)} custom-call(bf16[1,24,4096]{2,1,0:T(8,128)(2,1)} %q_hbm.1, bf16[1,24,4096]{2,1,0:T(8,128)(2,1)} %k_hbm.1, bf16[1,24,4096]{2,1,0:T(8,128)(2,1)} %v_hbm.1), custom_call_target="tpu_custom_call" | custom-call | tf_op jit(solution)/shard_map/pallas_call | solution.py:180
  2.0 31.7 %all_to_all.10 = bf16[32,3,24,128]{3,2,1,0:T(8,128)(2,1)S(1)} all-to-all(bf16[32,3,24,128]{3,2,1,0:T(8,128)(2,1)} %shard_map.64), channel_id=1, replica_groups=mesh['x'=4,'y_hi'=2,'y_lo'=4,'z'=8,'core'=2] {'y_lo','z'}, dimensions={0} | all-to-all | bytes 1179648 | tf_op jit(solution)/shard_map/all_to_all | solution.py:167
  33.8 4.4 %collective-permute-start = (bf16[2,768,128]{2,1,0:T(8,128)(2,1)S(1)}, bf16[2,768,128]{2,1,0:T(8,128)(2,1)S(1)}, u32[]{:S(2)}, u32[]{:S(2)}) collective-permute-start(bf16[2,768,128]{2,1,0:T(8,128)(2,1)S(1)} %bitcast.12), channel_id=1, source_target_pairs={{0,112},{16,96},{32,80},{48,64},{64,176},{80,160},{96,144},{112,12... | collective-permute-start | bytes 1179656 | tf_op jit(solution)/shard_map/ppermute | solution.py:164
  38.2 2.7 %collective-permute-start.1 = (bf16[768,128]{1,0:T(8,128)(2,1)S(1)}, bf16[768,128]{1,0:T(8,128)(2,1)S(1)}, u32[]{:S(2)}, u32[]{:S(2)}) collective-permute-start(bf16[768,128]{1,0:T(8,128)(2,1)S(1)} %bitcast.8), channel_id=1, source_target_pairs={{128,0},{192,64},{256,128},{320,192},{384,256},{448,320},{129,1},{... | collective-permute-start | bytes 589832 | tf_op jit(solution)/shard_map/ppermute | solution.py:171
  41.0 0.0 copy-start
  41.0 0.0 copy-start.1
  41.0 0.0 copy-start.2
  41.0 2.5 %all_gather.9.kv_ref = bf16[2,2,768,128]{3,2,1,0:T(8,128)(2,1)S(1)} all-gather(bf16[1,2,768,128]{3,2,1,0:T(8,128)(2,1)S(1)} %bitcast.13), channel_id=1, replica_groups=mesh['x'=4,'y_hi'=2,'y_lo'=4,'z'=8,'core'=2] {'core'}, dimensions={0}, use_global_device_ids=true | all-gather | bytes 1179648 | tf_op jit(solution)/shard_map/all_gather | solution.py:177
  43.5 0.0 copy-done
  43.5 0.0 copy-done.1
  43.5 0.0 copy-done.2
  43.5 3.0 %shard_map.65 = (f32[768,128]{1,0:T(8,128)S(1)}, f32[768,128]{1,0:T(8,128)S(1)}, f32[768,128]{1,0:T(8,128)S(1)}, f32[24,128]{1,0:T(8,128)S(1)}) custom-call(s32[8,8]{1,0:T(8,128)S(1)} %copy-done.1, s32[8]{0:T(128)S(1)} %copy-done.2, f32[8,4096]{1,0:T(8,128)S(1)} %copy-done, bf16[768,128]{1,0:T(8,128)(2,1)S(1)} %bitcast.9, ...), custom_call_target="tpu_custom_call" | custom-call | flops 1024 | bytes 1024 | tf_op jit(solution)/shard_map/pallas_call | solution.py:141
  46.6 0.0 collective-permute-done.1.q_ref
  46.6 2.4 %shard_map.67 = bf16[800,128]{1,0:T(8,128)(2,1)S(1)} custom-call(bf16[768,128]{1,0:T(8,128)(2,1)S(1)} %collective-permute-done.1.q_ref, bf16[2,2,768,128]{3,2,1,0:T(8,128)(2,1)S(1)} %all_gather.9.kv_ref), custom_call_target="tpu_custom_call" | custom-call | flops 1024 | bytes 1024 | tf_op jit(solution)/shard_map/pallas_call | solution.py:141
  49.0 1.3 %collective-permute-start.2 = (bf16[800,128]{1,0:T(8,128)(2,1)S(1)}, bf16[800,128]{1,0:T(8,128)(2,1)S(1)}, u32[]{:S(2)}, u32[]{:S(2)}) collective-permute-start(bf16[800,128]{1,0:T(8,128)(2,1)S(1)} %shard_map.67), channel_id=1, source_target_pairs={{0,128},{64,192},{128,256},{192,320},{256,384},{320,448},{1,129},{... | collective-permute-start | bytes 614408 | tf_op jit(solution)/shard_map/ppermute | solution.py:171
  50.3 5.9 %collective-permute-done = bf16[2,768,128]{2,1,0:T(8,128)(2,1)S(1)} collective-permute-done((bf16[2,768,128]{2,1,0:T(8,128)(2,1)S(1)}, bf16[2,768,128]{2,1,0:T(8,128)(2,1)S(1)}, u32[]{:S(2)}, u32[]{:S(2)}) %collective-permute-start) | collective-permute-done | bytes 393248 | tf_op jit(solution)/shard_map/ppermute | solution.py:164
  56.2 2.4 %all-gather = bf16[4,768,128]{2,1,0:T(8,128)(2,1)S(1)} all-gather(bf16[2,768,128]{2,1,0:T(8,128)(2,1)S(1)} %collective-permute-done), channel_id=2, replica_groups=mesh['x'=4,'y_hi'=2,'y_lo'=4,'z'=8,'core'=2] {'core'}, dimensions={0}, use_global_device_ids=true | all-gather | bytes 1179648 | tf_op jit(solution)/shard_map/all_gather | solution.py:177
  58.5 2.6 %shard_map.66 = (f32[768,128]{1,0:T(8,128)S(1)}, f32[768,128]{1,0:T(8,128)S(1)}, f32[768,128]{1,0:T(8,128)S(1)}) custom-call(f32[24,128]{1,0:T(8,128)S(1)} %get-tuple-element.16.aux_ref, bf16[768,128]{1,0:T(8,128)(2,1)S(1)} %bitcast.10, bf16[2,2,768,128]{3,2,1,0:T(8,128)(2,1)S(1)} %bitcast.7, f32[768,128]{1,0:T(8,128)S(1)} %get-tuple-element.20.m_in, ...), custom_call_target="tpu_custom_call" | custom-call | flops 1024 | bytes 1024 | tf_op jit(solution)/shard_map/pallas_call | solution.py:141
  61.1 0.0 collective-permute-done.2.part_ref
  61.1 0.3 shard_map.68
  61.5 17.7 %all_to_all.11.in_ref = bf16[32,24,128]{2,1,0:T(8,128)(2,1)S(1)} all-to-all(bf16[32,24,128]{2,1,0:T(8,128)(2,1)S(1)} %bitcast.11), channel_id=1, replica_groups=mesh['x'=4,'y_hi'=2,'y_lo'=4,'z'=8,'core'=2] {'y_lo','z'}, dimensions={0} | all-to-all | bytes 393216 | tf_op jit(solution)/shard_map/all_to_all | solution.py:167
  79.2 0.7 shard_map.69
  (3 shorter events, 0.1 us)
Async XLA Ops:
  33.8 22.4 %collective-permute-start = (bf16[2,768,128]{2,1,0:T(8,128)(2,1)S(1)}, bf16[2,768,128]{2,1,0:T(8,128)(2,1)S(1)}, u32[]{:S(2)}, u32[]{:S(2)}) collective-permute-start(bf16[2,768,128]{2,1,0:T(8,128)(2,1)S(1)} %bitcast.12), channel_id=1, source_target_pairs={{0,112},{16,96},{32,80},{48,64},{64,176},{80,160},{96,144},{112,12... | collective-permute-start | bytes 1179656 | tf_op jit(solution)/shard_map/ppermute | solution.py:164
  38.2 8.3 %collective-permute-start.1 = (bf16[768,128]{1,0:T(8,128)(2,1)S(1)}, bf16[768,128]{1,0:T(8,128)(2,1)S(1)}, u32[]{:S(2)}, u32[]{:S(2)}) collective-permute-start(bf16[768,128]{1,0:T(8,128)(2,1)S(1)} %bitcast.8), channel_id=1, source_target_pairs={{128,0},{192,64},{256,128},{320,192},{384,256},{448,320},{129,1},{... | collective-permute-start | bytes 589832 | tf_op jit(solution)/shard_map/ppermute | solution.py:171
  41.0 2.5 %copy-start = (f32[8,4096]{1,0:T(8,128)S(1)}, f32[8,4096]{1,0:T(8,128)}, u32[]{:S(2)}) copy-start(f32[8,4096]{1,0:T(8,128)} %gate_ref.1) | copy-start | bytes 393220
  41.0 2.5 %copy-start.1 = (s32[8,8]{1,0:T(8,128)S(1)}, s32[8,8]{1,0:T(8,128)}, u32[]{:S(2)}) copy-start(s32[8,8]{1,0:T(8,128)} %mask_ref.1) | copy-start | bytes 772
  41.0 2.5 %copy-start.2 = (s32[8]{0:T(128)S(1)}, s32[8]{0:T(128)}, u32[]{:S(2)}) copy-start(s32[8]{0:T(128)} %level_ref.1) | copy-start | bytes 100
  49.0 12.1 %collective-permute-start.2 = (bf16[800,128]{1,0:T(8,128)(2,1)S(1)}, bf16[800,128]{1,0:T(8,128)(2,1)S(1)}, u32[]{:S(2)}, u32[]{:S(2)}) collective-permute-start(bf16[800,128]{1,0:T(8,128)(2,1)S(1)} %shard_map.67), channel_id=1, source_target_pairs={{0,128},{64,192},{128,256},{192,320},{256,384},{320,448},{1,129},{... | collective-permute-start | bytes 614408 | tf_op jit(solution)/shard_map/ppermute | solution.py:171

commit v5 on v4

--- a/solution.py
+++ b/solution.py
@@ -12,6 +12,7 @@
 CHIPS = ("y_lo", "z")
 CONST = HD ** (-0.5) * 1.4426950408889634
 TILE = 384
+CHUNKS = 4
 VMEM_LIMIT = 24 * 1024 * 1024
 
 
@@ -116,23 +117,36 @@
     return jnp.where(lax.axis_index("y_hi") > 0, line - 1 - at, at) * depth + z
 
 
-def split_heads(q_hbm, k_hbm, v_hbm, out_ref, *held_and_sems):
-    held, sems = held_and_sems[:3], held_and_sems[3:]
-    copies = [
-        pltpu.make_async_copy(source, target, sem)
-        for source, target, sem in zip((q_hbm, k_hbm, v_hbm), held, sems)
-    ]
+def split_heads(q_hbm, k_hbm, v_hbm, out_ref, held, sems):
+    wide = q_hbm.shape[2] // CHUNKS
+    copies = []
+    for i, source in enumerate((q_hbm, k_hbm, v_hbm)):
+        for c in range(CHUNKS):
+            at = pl.ds(c * wide, wide)
+            copies.append(
+                pltpu.make_async_copy(source.at[0, :, at], held.at[i, :, at], sems.at[i * CHUNKS + c])
+            )
     for copy in copies:
         copy.start()
-    for i, (copy, ref) in enumerate(zip(copies, held)):
+    each = out_ref.shape[0] // CHUNKS
+    for i in range(3):
+        for c in range(CHUNKS):
+            copies[i * CHUNKS + c].wait()
+            for h in range(c * each, (c + 1) * each):
+                out_ref[placed(h), i] = held[i, :, h * HD : (h + 1) * HD]
+
+
+def join_heads(in_ref, out_hbm, held, sems):
+    each = in_ref.shape[0] // CHUNKS
+    copies = []
+    for c in range(CHUNKS):
+        for h in range(c * each, (c + 1) * each):
+            held[:, h * HD : (h + 1) * HD] = in_ref[placed(h)]
+        at = pl.ds(c * each * HD, each * HD)
+        copies.append(pltpu.make_async_copy(held.at[:, at], out_hbm.at[0, :, at], sems.at[c]))
+        copies[-1].start()
+    for copy in copies:
         copy.wait()
-        for h in range(out_ref.shape[0]):
-            out_ref[placed(h), i] = ref[0, :, h * HD : (h + 1) * HD]
-
-
-def join_heads(in_ref, out_ref):
-    for h in range(in_ref.shape[0]):
-        out_ref[0, :, h * HD : (h + 1) * HD] = in_ref[placed(h)]
 
 
 def call(kernel, out_shape, scalars, *arrays):
@@ -182,7 +196,10 @@
         out_shape=by_head,
         in_specs=[pl.BlockSpec(memory_space=pltpu.HBM)] * 3,
         out_specs=pl.BlockSpec(memory_space=pltpu.VMEM),
-        scratch_shapes=[pltpu.VMEM(queries.shape, queries.dtype)] * 3 + [pltpu.SemaphoreType.DMA] * 3,
+        scratch_shapes=[
+            pltpu.VMEM((3, local, heads * HD), queries.dtype),
+            pltpu.SemaphoreType.DMA((3 * CHUNKS,)),
+        ],
         compiler_params=pltpu.CompilerParams(vmem_limit_bytes=60 * 1024 * 1024),
     )(queries, key_rows, value_rows)
     got = exchange(mixed)
@@ -195,17 +212,22 @@
     kv1 = to_next(kv)
     later_q = moved(q, -2)
     kv0 = both_cores(kv)
+    (served,) = call(served_block, [part], (), later_q, kv0)
     *state, aux = call(own_block, [stat, stat, stat, aux], (block_mask, noise_level), gate_table, q, kv0)
-    later_q, *state = lax.optimization_barrier((later_q, *state))
-    (served,) = call(served_block, [part], (), later_q, kv0)
     part2 = moved(served, 2)
     kv1 = both_cores(kv1)
     state = call(earlier_block, [stat, stat, stat], (), aux, q, kv1, *state)
     (out,) = call(join, [jax.ShapeDtypeStruct((rows, HD), jnp.bfloat16)], (), aux, *state, part2)
 
     back = exchange(out.reshape(heads, local, HD))
-    (attended,) = call(join_heads, [jax.ShapeDtypeStruct(queries.shape, queries.dtype)], (), back)
-    return attended
+    return pl.pallas_call(
+        join_heads,
+        out_shape=jax.ShapeDtypeStruct(queries.shape, queries.dtype),
+        in_specs=[pl.BlockSpec(memory_space=pltpu.VMEM)],
+        out_specs=pl.BlockSpec(memory_space=pltpu.HBM),
+        scratch_shapes=[pltpu.VMEM((local, heads * HD), queries.dtype), pltpu.SemaphoreType.DMA((CHUNKS,))],
+        compiler_params=pltpu.CompilerParams(vmem_limit_bytes=VMEM_LIMIT),
+    )(back)
 
 
 def solution(mesh):

time: 80.3 us -> 80.3 us (level)
    ppermute x2, waiting for transfers between devices: 0.01 us -> 1.56 us  [moved(): return lax.ppermute(block, SPAN, route)]
    ppermute x1, waiting for transfers between devices: 5.88 us -> 4.5 us  [to_next(): return lax.ppermute(block, SPAN + ('y_lo',), route)]
    pallas_call x5 -> x4, Pallas kernels: 9.07 us -> 8.34 us  [call(): pl.pallas_call(kernel, out_shape=out_shape, in_specs=[smem] * len(scalars...]
  transfers between devices with their start and end apart: 3 -> 3, of which waited for: 1 -> 2; matrix products, arithmetic and copies ran while one was open for 0% -> 0% of each run, Pallas kernels for 10% -> 10%
where the time goes in v5:
time: 80.3 us; the launch traced here: 79.9 us
  blocking collectives  54.2 us (67%)
  Pallas kernels  11 us (14%)
  starting transfers between devices  8.44 us (11%)
  waiting for transfers between devices  6.06 us (8%)
    all_to_all x2, blocking collectives, exchange(): return lax.all_to_all(block, CHIPS, split_axis=0, concat_axis=0, tiled=True)  49.5 us
    pallas_call x4, Pallas kernels, call(): pl.pallas_call(kernel, out_shape=out_shape, in_specs=[smem] * len(scalars...  8.34 us
    all_gather x2, blocking collectives, both_cores(): return lax.all_gather(block, 'core')  4.73 us
    ppermute x1, waiting for transfers between devices, to_next(): return lax.ppermute(block, SPAN + ('y_lo',), route)  4.5 us
    ppermute x1, starting transfers between devices, to_next(): return lax.ppermute(block, SPAN + ('y_lo',), route)  4.4 us
    ppermute x2, starting transfers between devices, moved(): return lax.ppermute(block, SPAN, route)  4.04 us
    pallas_call x1, Pallas kernels, on_device(): pl.pallas_call(split_heads, out_shape=by_head, in_specs=[pl.BlockSpec(mem...  1.98 us
  transfers between devices with their start and end apart: 3, of which 2 were waited for; matrix products, arithmetic and copies ran while one was open for 0% of the time, Pallas kernels for 10%

profile of v5, /device:TPU:6, one launch (start us, length us, event | category | flops | bytes accessed | tf_op | source)
XLA Modules:
  0.0 79.9 jit_solution(15060657270273664365)
XLA Ops:
  0.0 2.0 %shard_map.64 = bf16[32,3,24,128]{3,2,1,0:T(8,128)(2,1)} custom-call(bf16[1,24,4096]{2,1,0:T(8,128)(2,1)} %q_hbm.1, bf16[1,24,4096]{2,1,0:T(8,128)(2,1)} %k_hbm.1, bf16[1,24,4096]{2,1,0:T(8,128)(2,1)} %v_hbm.1), custom_call_target="tpu_custom_call" | custom-call | tf_op jit(solution)/shard_map/pallas_call | solution.py:194
  2.0 31.7 %all_to_all.10 = bf16[32,3,24,128]{3,2,1,0:T(8,128)(2,1)S(1)} all-to-all(bf16[32,3,24,128]{3,2,1,0:T(8,128)(2,1)} %shard_map.64), channel_id=1, replica_groups=mesh['x'=4,'y_hi'=2,'y_lo'=4,'z'=8,'core'=2] {'y_lo','z'}, dimensions={0} | all-to-all | bytes 1179648 | tf_op jit(solution)/shard_map/all_to_all | solution.py:181
  33.8 4.4 %collective-permute-start = (bf16[2,768,128]{2,1,0:T(8,128)(2,1)S(1)}, bf16[2,768,128]{2,1,0:T(8,128)(2,1)S(1)}, u32[]{:S(2)}, u32[]{:S(2)}) collective-permute-start(bf16[2,768,128]{2,1,0:T(8,128)(2,1)S(1)} %bitcast.12), channel_id=1, source_target_pairs={{0,112},{16,96},{32,80},{48,64},{64,176},{80,160},{96,144},{112,12... | collective-permute-start | bytes 1179656 | tf_op jit(solution)/shard_map/ppermute | solution.py:178
  38.3 2.7 %collective-permute-start.1 = (bf16[768,128]{1,0:T(8,128)(2,1)S(1)}, bf16[768,128]{1,0:T(8,128)(2,1)S(1)}, u32[]{:S(2)}, u32[]{:S(2)}) collective-permute-start(bf16[768,128]{1,0:T(8,128)(2,1)S(1)} %bitcast.8), channel_id=1, source_target_pairs={{128,0},{192,64},{256,128},{320,192},{384,256},{448,320},{129,1},{... | collective-permute-start | bytes 589832 | tf_op jit(solution)/shard_map/ppermute | solution.py:185
  41.0 2.4 %all_gather.9.kv_ref = bf16[2,2,768,128]{3,2,1,0:T(8,128)(2,1)S(1)} all-gather(bf16[1,2,768,128]{3,2,1,0:T(8,128)(2,1)S(1)} %bitcast.13), channel_id=1, replica_groups=mesh['x'=4,'y_hi'=2,'y_lo'=4,'z'=8,'core'=2] {'core'}, dimensions={0}, use_global_device_ids=true | all-gather | bytes 1179648 | tf_op jit(solution)/shard_map/all_gather | solution.py:191
  43.4 0.0 copy-start
  43.4 0.0 copy-start.1
  43.4 0.0 copy-start.2
  43.4 1.6 %collective-permute-done.1.q_ref = bf16[768,128]{1,0:T(8,128)(2,1)S(1)} collective-permute-done((bf16[768,128]{1,0:T(8,128)(2,1)S(1)}, bf16[768,128]{1,0:T(8,128)(2,1)S(1)}, u32[]{:S(2)}, u32[]{:S(2)}) %collective-permute-start.1) | collective-permute-done | bytes 196640 | tf_op jit(solution)/shard_map/ppermute | solution.py:185
  44.9 2.4 %shard_map.67 = bf16[800,128]{1,0:T(8,128)(2,1)S(1)} custom-call(bf16[768,128]{1,0:T(8,128)(2,1)S(1)} %collective-permute-done.1.q_ref, bf16[2,2,768,128]{3,2,1,0:T(8,128)(2,1)S(1)} %all_gather.9.kv_ref), custom_call_target="tpu_custom_call" | custom-call | flops 1024 | bytes 1024 | tf_op jit(solution)/shard_map/pallas_call | solution.py:155
  47.3 1.3 %collective-permute-start.2 = (bf16[800,128]{1,0:T(8,128)(2,1)S(1)}, bf16[800,128]{1,0:T(8,128)(2,1)S(1)}, u32[]{:S(2)}, u32[]{:S(2)}) collective-permute-start(bf16[800,128]{1,0:T(8,128)(2,1)S(1)} %shard_map.67), channel_id=1, source_target_pairs={{0,128},{64,192},{128,256},{192,320},{256,384},{320,448},{1,129},{... | collective-permute-start | bytes 614408 | tf_op jit(solution)/shard_map/ppermute | solution.py:185
  48.6 0.0 copy-done
  48.7 0.0 copy-done.1
  48.7 0.0 copy-done.2
  48.7 3.0 %shard_map.65 = (f32[768,128]{1,0:T(8,128)S(1)}, f32[768,128]{1,0:T(8,128)S(1)}, f32[768,128]{1,0:T(8,128)S(1)}, f32[24,128]{1,0:T(8,128)S(1)}) custom-call(s32[8,8]{1,0:T(8,128)S(1)} %copy-done.1, s32[8]{0:T(128)S(1)} %copy-done.2, f32[8,4096]{1,0:T(8,128)S(1)} %copy-done, bf16[768,128]{1,0:T(8,128)(2,1)S(1)} %bitcast.9, ...), custom_call_target="tpu_custom_call" | custom-call | flops 1024 | bytes 1024 | tf_op jit(solution)/shard_map/pallas_call | solution.py:155
  51.7 4.5 %collective-permute-done = bf16[2,768,128]{2,1,0:T(8,128)(2,1)S(1)} collective-permute-done((bf16[2,768,128]{2,1,0:T(8,128)(2,1)S(1)}, bf16[2,768,128]{2,1,0:T(8,128)(2,1)S(1)}, u32[]{:S(2)}, u32[]{:S(2)}) %collective-permute-start) | collective-permute-done | bytes 393248 | tf_op jit(solution)/shard_map/ppermute | solution.py:178
  56.2 2.4 %all-gather = bf16[4,768,128]{2,1,0:T(8,128)(2,1)S(1)} all-gather(bf16[2,768,128]{2,1,0:T(8,128)(2,1)S(1)} %collective-permute-done), channel_id=2, replica_groups=mesh['x'=4,'y_hi'=2,'y_lo'=4,'z'=8,'core'=2] {'core'}, dimensions={0}, use_global_device_ids=true | all-gather | bytes 1179648 | tf_op jit(solution)/shard_map/all_gather | solution.py:191
  58.6 2.6 %shard_map.66 = (f32[768,128]{1,0:T(8,128)S(1)}, f32[768,128]{1,0:T(8,128)S(1)}, f32[768,128]{1,0:T(8,128)S(1)}) custom-call(f32[24,128]{1,0:T(8,128)S(1)} %get-tuple-element.12.aux_ref, bf16[768,128]{1,0:T(8,128)(2,1)S(1)} %bitcast.10, bf16[2,2,768,128]{3,2,1,0:T(8,128)(2,1)S(1)} %bitcast.7, f32[768,128]{1,0:T(8,128)S(1)} %get-tuple-element.13.m_in, ...), custom_call_target="tpu_custom_call" | custom-call | flops 1024 | bytes 1024 | tf_op jit(solution)/shard_map/pallas_call | solution.py:155
  61.1 0.0 collective-permute-done.2.part_ref
  61.1 0.3 shard_map.68
  61.5 17.7 %all_to_all.11.in_ref = bf16[32,24,128]{2,1,0:T(8,128)(2,1)S(1)} all-to-all(bf16[32,24,128]{2,1,0:T(8,128)(2,1)S(1)} %bitcast.11), channel_id=1, replica_groups=mesh['x'=4,'y_hi'=2,'y_lo'=4,'z'=8,'core'=2] {'y_lo','z'}, dimensions={0} | all-to-all | bytes 393216 | tf_op jit(solution)/shard_map/all_to_all | solution.py:181
  79.2 0.7 shard_map.69
  (3 shorter events, 0.1 us)
Async XLA Ops:
  33.8 22.4 %collective-permute-start = (bf16[2,768,128]{2,1,0:T(8,128)(2,1)S(1)}, bf16[2,768,128]{2,1,0:T(8,128)(2,1)S(1)}, u32[]{:S(2)}, u32[]{:S(2)}) collective-permute-start(bf16[2,768,128]{2,1,0:T(8,128)(2,1)S(1)} %bitcast.12), channel_id=1, source_target_pairs={{0,112},{16,96},{32,80},{48,64},{64,176},{80,160},{96,144},{112,12... | collective-permute-start | bytes 1179656 | tf_op jit(solution)/shard_map/ppermute | solution.py:178
  38.3 6.7 %collective-permute-start.1 = (bf16[768,128]{1,0:T(8,128)(2,1)S(1)}, bf16[768,128]{1,0:T(8,128)(2,1)S(1)}, u32[]{:S(2)}, u32[]{:S(2)}) collective-permute-start(bf16[768,128]{1,0:T(8,128)(2,1)S(1)} %bitcast.8), channel_id=1, source_target_pairs={{128,0},{192,64},{256,128},{320,192},{384,256},{448,320},{129,1},{... | collective-permute-start | bytes 589832 | tf_op jit(solution)/shard_map/ppermute | solution.py:185
  43.4 5.3 %copy-start = (f32[8,4096]{1,0:T(8,128)S(1)}, f32[8,4096]{1,0:T(8,128)}, u32[]{:S(2)}) copy-start(f32[8,4096]{1,0:T(8,128)} %gate_ref.1) | copy-start | bytes 393220
  43.4 5.3 %copy-start.1 = (s32[8,8]{1,0:T(8,128)S(1)}, s32[8,8]{1,0:T(8,128)}, u32[]{:S(2)}) copy-start(s32[8,8]{1,0:T(8,128)} %mask_ref.1) | copy-start | bytes 772
  43.4 5.3 %copy-start.2 = (s32[8]{0:T(128)S(1)}, s32[8]{0:T(128)}, u32[]{:S(2)}) copy-start(s32[8]{0:T(128)} %level_ref.1) | copy-start | bytes 100
  47.3 13.8 %collective-permute-start.2 = (bf16[800,128]{1,0:T(8,128)(2,1)S(1)}, bf16[800,128]{1,0:T(8,128)(2,1)S(1)}, u32[]{:S(2)}, u32[]{:S(2)}) collective-permute-start(bf16[800,128]{1,0:T(8,128)(2,1)S(1)} %shard_map.67), channel_id=1, source_target_pairs={{0,128},{64,192},{128,256},{192,320},{256,384},{320,448},{1,129},{... | collective-permute-start | bytes 614408 | tf_op jit(solution)/shard_map/ppermute | solution.py:185

commit v6 on v5

--- a/solution.py
+++ b/solution.py
@@ -74,40 +74,35 @@
     out_ref[pl.ds(rows, 32), :] = pieces.astype(jnp.bfloat16)
 
 
-def earlier_block(aux_ref, q_ref, kv_ref, m_in, l_in, a_in, m_out, l_out, a_out):
-    opened = aux_ref[0:1, :1] > 0.5
-    for t in range(q_ref.shape[0] // TILE):
-        at = pl.ds(t * TILE, TILE)
-        before = m_in[at, :1]
-
-        def joined(own):
-            top = jnp.where(opened, jnp.maximum(own, before), before)
-            return top, jnp.where(opened, top, 1e30)
-
-        top, total, heard = weigh(q_ref[at, :], (kv_ref.at[0], kv_ref.at[1]), joined, CONST)
-        shrink = jnp.exp2((before - top) * CONST)
-        m_out[at, :] = jnp.broadcast_to(top, (TILE, HD))
-        l_out[at, :] = jnp.broadcast_to(total + l_in[at, :1] * shrink, (TILE, HD))
-        a_out[at, :] = heard + a_in[at, :] * shrink
-
-
-def join(aux_ref, m_in, l_in, a_in, part_ref, out_ref):
-    rows = m_in.shape[0]
-    opened = aux_ref[8:9, :1] > 0.5
+def last_block(aux_ref, q_ref, kv_ref, m_in, l_in, a_in, part_ref, out_ref):
+    rows = q_ref.shape[0]
+    opened1 = aux_ref[0:1, :1] > 0.5
+    opened2 = aux_ref[8:9, :1] > 0.5
     gate = aux_ref[16:17, :]
     eye = diagonal()
     pieces = part_ref[pl.ds(rows, 32), :].astype(jnp.float32)
     level = pieces[0:8] + pieces[8:16] + pieces[16:24]
-    for t in range(rows // HD):
-        at = pl.ds(t * HD, HD)
-        before = m_in[at, :]
-        served = jnp.where(eye, level[t : t + 1], 0.0).sum(axis=1, keepdims=True)
-        served = jnp.where(opened, served, before)
-        top = jnp.maximum(before, served)
+    for t in range(rows // TILE):
+        at = pl.ds(t * TILE, TILE)
+        before = m_in[at, :1]
+        served = jnp.concatenate(
+            [
+                jnp.where(eye, level[j : j + 1], 0.0).sum(axis=1, keepdims=True)
+                for j in range(t * TILE // HD, (t + 1) * TILE // HD)
+            ],
+            axis=0,
+        )
+        known = jnp.where(opened2, jnp.maximum(before, served), before)
+
+        def joined(own):
+            top = jnp.where(opened1, jnp.maximum(own, known), known)
+            return top, jnp.where(opened1, top, 1e30)
+
+        top, total, heard = weigh(q_ref[at, :], (kv_ref.at[0], kv_ref.at[1]), joined, CONST)
         shrink = jnp.exp2((before - top) * CONST)
-        share = jnp.where(opened, jnp.exp2((served - top) * CONST), 0.0)
-        total = l_in[at, :] * shrink + share
-        heard = a_in[at, :] * shrink + part_ref[at, :].astype(jnp.float32) * share
+        share = jnp.where(opened2, jnp.exp2((jnp.where(opened2, served, top) - top) * CONST), 0.0)
+        total = total + l_in[at, :1] * shrink + share
+        heard = heard + a_in[at, :] * shrink + part_ref[at, :].astype(jnp.float32) * share
         out_ref[at, :] = (heard / total * gate).astype(jnp.bfloat16)
 
 
@@ -216,8 +211,9 @@
     *state, aux = call(own_block, [stat, stat, stat, aux], (block_mask, noise_level), gate_table, q, kv0)
     part2 = moved(served, 2)
     kv1 = both_cores(kv1)
-    state = call(earlier_block, [stat, stat, stat], (), aux, q, kv1, *state)
-    (out,) = call(join, [jax.ShapeDtypeStruct((rows, HD), jnp.bfloat16)], (), aux, *state, part2)
+    (out,) = call(
+        last_block, [jax.ShapeDtypeStruct((rows, HD), jnp.bfloat16)], (), aux, q, kv1, *state, part2
+    )
 
     back = exchange(out.reshape(heads, local, HD))
     return pl.pallas_call(

time: 80.3 us -> 81.8 us (1.019)
  waiting for transfers between devices: 6.06 us -> 7.97 us
    ppermute x2, waiting for transfers between devices: 1.56 us -> 3.48 us  [moved(): return lax.ppermute(block, SPAN, route)]
    pallas_call x4 -> x3, Pallas kernels: 8.34 us -> 8.05 us  [call(): pl.pallas_call(kernel, out_shape=out_shape, in_specs=[smem] * len(scalars...]
  transfers between devices with their start and end apart: 3 -> 3, of which waited for: 2 -> 3; matrix products, arithmetic and copies ran while one was open for 0% -> 0% of each run, Pallas kernels for 10% -> 7%
where the time goes in v6:
time: 81.8 us; the launch traced here: 81.4 us
  blocking collectives  54 us (66%)
  Pallas kernels  10.8 us (13%)
  starting transfers between devices  8.44 us (10%)
  waiting for transfers between devices  7.97 us (10%)
    all_to_all x2, blocking collectives, exchange(): return lax.all_to_all(block, CHIPS, split_axis=0, concat_axis=0, tiled=True)  49.3 us
    pallas_call x3, Pallas kernels, call(): pl.pallas_call(kernel, out_shape=out_shape, in_specs=[smem] * len(scalars...  8.05 us
    all_gather x2, blocking collectives, both_cores(): return lax.all_gather(block, 'core')  4.73 us
    ppermute x1, waiting for transfers between devices, to_next(): return lax.ppermute(block, SPAN + ('y_lo',), route)  4.49 us
    ppermute x1, starting transfers between devices, to_next(): return lax.ppermute(block, SPAN + ('y_lo',), route)  4.4 us
    ppermute x2, starting transfers between devices, moved(): return lax.ppermute(block, SPAN, route)  4.04 us
    ppermute x2, waiting for transfers between devices, moved(): return lax.ppermute(block, SPAN, route)  3.48 us
    pallas_call x1, Pallas kernels, on_device(): pl.pallas_call(split_heads, out_shape=by_head, in_specs=[pl.BlockSpec(mem...  2 us
  transfers between devices with their start and end apart: 3, of which 3 were waited for; matrix products, arithmetic and copies ran while one was open for 0% of the time, Pallas kernels for 7%

profile of v6, /device:TPU:6, one launch (start us, length us, event | category | flops | bytes accessed | tf_op | source)
XLA Modules:
  0.0 81.4 jit_solution(9853947151704047105)
XLA Ops:
  0.0 2.0 %shard_map.64 = bf16[32,3,24,128]{3,2,1,0:T(8,128)(2,1)} custom-call(bf16[1,24,4096]{2,1,0:T(8,128)(2,1)} %q_hbm.1, bf16[1,24,4096]{2,1,0:T(8,128)(2,1)} %k_hbm.1, bf16[1,24,4096]{2,1,0:T(8,128)(2,1)} %v_hbm.1), custom_call_target="tpu_custom_call" | custom-call | tf_op jit(solution)/shard_map/pallas_call | solution.py:189
  2.0 31.7 %all_to_all.10 = bf16[32,3,24,128]{3,2,1,0:T(8,128)(2,1)S(1)} all-to-all(bf16[32,3,24,128]{3,2,1,0:T(8,128)(2,1)} %shard_map.64), channel_id=1, replica_groups=mesh['x'=4,'y_hi'=2,'y_lo'=4,'z'=8,'core'=2] {'y_lo','z'}, dimensions={0} | all-to-all | bytes 1179648 | tf_op jit(solution)/shard_map/all_to_all | solution.py:176
  33.8 4.4 %collective-permute-start = (bf16[2,768,128]{2,1,0:T(8,128)(2,1)S(1)}, bf16[2,768,128]{2,1,0:T(8,128)(2,1)S(1)}, u32[]{:S(2)}, u32[]{:S(2)}) collective-permute-start(bf16[2,768,128]{2,1,0:T(8,128)(2,1)S(1)} %bitcast.12), channel_id=1, source_target_pairs={{0,112},{16,96},{32,80},{48,64},{64,176},{80,160},{96,144},{112,12... | collective-permute-start | bytes 1179656 | tf_op jit(solution)/shard_map/ppermute | solution.py:173
  38.3 2.7 %collective-permute-start.1 = (bf16[768,128]{1,0:T(8,128)(2,1)S(1)}, bf16[768,128]{1,0:T(8,128)(2,1)S(1)}, u32[]{:S(2)}, u32[]{:S(2)}) collective-permute-start(bf16[768,128]{1,0:T(8,128)(2,1)S(1)} %bitcast.8), channel_id=1, source_target_pairs={{128,0},{192,64},{256,128},{320,192},{384,256},{448,320},{129,1},{... | collective-permute-start | bytes 589832 | tf_op jit(solution)/shard_map/ppermute | solution.py:180
  41.0 2.4 %all_gather.9.kv_ref = bf16[2,2,768,128]{3,2,1,0:T(8,128)(2,1)S(1)} all-gather(bf16[1,2,768,128]{3,2,1,0:T(8,128)(2,1)S(1)} %bitcast.13), channel_id=1, replica_groups=mesh['x'=4,'y_hi'=2,'y_lo'=4,'z'=8,'core'=2] {'core'}, dimensions={0}, use_global_device_ids=true | all-gather | bytes 1179648 | tf_op jit(solution)/shard_map/all_gather | solution.py:186
  43.4 0.0 copy-start
  43.4 0.0 copy-start.1
  43.4 0.0 copy-start.2
  43.4 1.6 %collective-permute-done.1.q_ref = bf16[768,128]{1,0:T(8,128)(2,1)S(1)} collective-permute-done((bf16[768,128]{1,0:T(8,128)(2,1)S(1)}, bf16[768,128]{1,0:T(8,128)(2,1)S(1)}, u32[]{:S(2)}, u32[]{:S(2)}) %collective-permute-start.1) | collective-permute-done | bytes 196640 | tf_op jit(solution)/shard_map/ppermute | solution.py:180
  44.9 2.4 %shard_map.66 = bf16[800,128]{1,0:T(8,128)(2,1)S(1)} custom-call(bf16[768,128]{1,0:T(8,128)(2,1)S(1)} %collective-permute-done.1.q_ref, bf16[2,2,768,128]{3,2,1,0:T(8,128)(2,1)S(1)} %all_gather.9.kv_ref), custom_call_target="tpu_custom_call" | custom-call | flops 1024 | bytes 1024 | tf_op jit(solution)/shard_map/pallas_call | solution.py:150
  47.4 1.3 %collective-permute-start.2 = (bf16[800,128]{1,0:T(8,128)(2,1)S(1)}, bf16[800,128]{1,0:T(8,128)(2,1)S(1)}, u32[]{:S(2)}, u32[]{:S(2)}) collective-permute-start(bf16[800,128]{1,0:T(8,128)(2,1)S(1)} %shard_map.66), channel_id=1, source_target_pairs={{0,128},{64,192},{128,256},{192,320},{256,384},{320,448},{1,129},{... | collective-permute-start | bytes 614408 | tf_op jit(solution)/shard_map/ppermute | solution.py:180
  48.7 0.0 copy-done
  48.7 0.0 copy-done.1
  48.7 0.0 copy-done.2
  48.7 3.0 %shard_map.65 = (f32[768,128]{1,0:T(8,128)S(1)}, f32[768,128]{1,0:T(8,128)S(1)}, f32[768,128]{1,0:T(8,128)S(1)}, f32[24,128]{1,0:T(8,128)S(1)}) custom-call(s32[8,8]{1,0:T(8,128)S(1)} %copy-done.1, s32[8]{0:T(128)S(1)} %copy-done.2, f32[8,4096]{1,0:T(8,128)S(1)} %copy-done, bf16[768,128]{1,0:T(8,128)(2,1)S(1)} %bitcast.9, ...), custom_call_target="tpu_custom_call" | custom-call | flops 1024 | bytes 1024 | tf_op jit(solution)/shard_map/pallas_call | solution.py:150
  51.7 4.5 %collective-permute-done = bf16[2,768,128]{2,1,0:T(8,128)(2,1)S(1)} collective-permute-done((bf16[2,768,128]{2,1,0:T(8,128)(2,1)S(1)}, bf16[2,768,128]{2,1,0:T(8,128)(2,1)S(1)}, u32[]{:S(2)}, u32[]{:S(2)}) %collective-permute-start) | collective-permute-done | bytes 393248 | tf_op jit(solution)/shard_map/ppermute | solution.py:173
  56.2 2.4 %all-gather = bf16[4,768,128]{2,1,0:T(8,128)(2,1)S(1)} all-gather(bf16[2,768,128]{2,1,0:T(8,128)(2,1)S(1)} %collective-permute-done), channel_id=2, replica_groups=mesh['x'=4,'y_hi'=2,'y_lo'=4,'z'=8,'core'=2] {'core'}, dimensions={0}, use_global_device_ids=true | all-gather | bytes 1179648 | tf_op jit(solution)/shard_map/all_gather | solution.py:186
  58.6 1.9 %collective-permute-done.2.part_ref = bf16[800,128]{1,0:T(8,128)(2,1)S(1)} collective-permute-done((bf16[800,128]{1,0:T(8,128)(2,1)S(1)}, bf16[800,128]{1,0:T(8,128)(2,1)S(1)}, u32[]{:S(2)}, u32[]{:S(2)}) %collective-permute-start.2) | collective-permute-done | bytes 204832 | tf_op jit(solution)/shard_map/ppermute | solution.py:180
  60.5 2.6 %shard_map.67 = bf16[768,128]{1,0:T(8,128)(2,1)S(1)} custom-call(f32[24,128]{1,0:T(8,128)S(1)} %get-tuple-element.9.aux_ref, bf16[768,128]{1,0:T(8,128)(2,1)S(1)} %bitcast.10, bf16[2,2,768,128]{3,2,1,0:T(8,128)(2,1)S(1)} %bitcast.7, f32[768,128]{1,0:T(8,128)S(1)} %get-tuple-element.10.m_in, f32[768,128]{1,0:T(8,128)S(1)} %get-tuple-element.11.l_in, ...), custom_call_target="tpu_custom_call" | custom-call | flops 1024 | bytes 1024 | tf_op jit(solution)/shard_map/pallas_call | solution.py:150
  63.1 17.6 %all_to_all.11.in_ref = bf16[32,24,128]{2,1,0:T(8,128)(2,1)S(1)} all-to-all(bf16[32,24,128]{2,1,0:T(8,128)(2,1)S(1)} %bitcast.11), channel_id=1, replica_groups=mesh['x'=4,'y_hi'=2,'y_lo'=4,'z'=8,'core'=2] {'y_lo','z'}, dimensions={0} | all-to-all | bytes 393216 | tf_op jit(solution)/shard_map/all_to_all | solution.py:176
  80.7 0.7 shard_map.68
  (3 shorter events, 0.1 us)
Async XLA Ops:
  33.8 22.4 %collective-permute-start = (bf16[2,768,128]{2,1,0:T(8,128)(2,1)S(1)}, bf16[2,768,128]{2,1,0:T(8,128)(2,1)S(1)}, u32[]{:S(2)}, u32[]{:S(2)}) collective-permute-start(bf16[2,768,128]{2,1,0:T(8,128)(2,1)S(1)} %bitcast.12), channel_id=1, source_target_pairs={{0,112},{16,96},{32,80},{48,64},{64,176},{80,160},{96,144},{112,12... | collective-permute-start | bytes 1179656 | tf_op jit(solution)/shard_map/ppermute | solution.py:173
  38.3 6.7 %collective-permute-start.1 = (bf16[768,128]{1,0:T(8,128)(2,1)S(1)}, bf16[768,128]{1,0:T(8,128)(2,1)S(1)}, u32[]{:S(2)}, u32[]{:S(2)}) collective-permute-start(bf16[768,128]{1,0:T(8,128)(2,1)S(1)} %bitcast.8), channel_id=1, source_target_pairs={{128,0},{192,64},{256,128},{320,192},{384,256},{448,320},{129,1},{... | collective-permute-start | bytes 589832 | tf_op jit(solution)/shard_map/ppermute | solution.py:180
  43.4 5.3 %copy-start = (f32[8,4096]{1,0:T(8,128)S(1)}, f32[8,4096]{1,0:T(8,128)}, u32[]{:S(2)}) copy-start(f32[8,4096]{1,0:T(8,128)} %gate_ref.1) | copy-start | bytes 393220
  43.4 5.3 %copy-start.1 = (s32[8,8]{1,0:T(8,128)S(1)}, s32[8,8]{1,0:T(8,128)}, u32[]{:S(2)}) copy-start(s32[8,8]{1,0:T(8,128)} %mask_ref.1) | copy-start | bytes 772
  43.4 5.3 %copy-start.2 = (s32[8]{0:T(128)S(1)}, s32[8]{0:T(128)}, u32[]{:S(2)}) copy-start(s32[8]{0:T(128)} %level_ref.1) | copy-start | bytes 100
  47.4 13.1 %collective-permute-start.2 = (bf16[800,128]{1,0:T(8,128)(2,1)S(1)}, bf16[800,128]{1,0:T(8,128)(2,1)S(1)}, u32[]{:S(2)}, u32[]{:S(2)}) collective-permute-start(bf16[800,128]{1,0:T(8,128)(2,1)S(1)} %shard_map.66), channel_id=1, source_target_pairs={{0,128},{64,192},{128,256},{192,320},{256,384},{320,448},{1,129},{... | collective-permute-start | bytes 614408 | tf_op jit(solution)/shard_map/ppermute | solution.py:180

commit v7 on v5

--- a/solution.py
+++ b/solution.py
@@ -12,7 +12,7 @@
 CHIPS = ("y_lo", "z")
 CONST = HD ** (-0.5) * 1.4426950408889634
 TILE = 384
-CHUNKS = 4
+CHUNKS = 2
 VMEM_LIMIT = 24 * 1024 * 1024
 
 

time: 80.3 us -> 80.3 us (level)
  no operation moved by 1% of the time
where the time goes in v7:
time: 80.3 us; the launch traced here: 80 us
  blocking collectives  54.2 us (67%)
  Pallas kernels  11.1 us (14%)
  starting transfers between devices  8.44 us (11%)
  waiting for transfers between devices  6.06 us (8%)
    all_to_all x2, blocking collectives, exchange(): return lax.all_to_all(block, CHIPS, split_axis=0, concat_axis=0, tiled=True)  49.5 us
    pallas_call x4, Pallas kernels, call(): pl.pallas_call(kernel, out_shape=out_shape, in_specs=[smem] * len(scalars...  8.34 us
    all_gather x2, blocking collectives, both_cores(): return lax.all_gather(block, 'core')  4.73 us
    ppermute x1, waiting for transfers between devices, to_next(): return lax.ppermute(block, SPAN + ('y_lo',), route)  4.5 us
    ppermute x1, starting transfers between devices, to_next(): return lax.ppermute(block, SPAN + ('y_lo',), route)  4.4 us
    ppermute x2, starting transfers between devices, moved(): return lax.ppermute(block, SPAN, route)  4.04 us
    pallas_call x1, Pallas kernels, on_device(): pl.pallas_call(split_heads, out_shape=by_head, in_specs=[pl.BlockSpec(mem...  2 us
  transfers between devices with their start and end apart: 3, of which 2 were waited for; matrix products, arithmetic and copies ran while one was open for 0% of the time, Pallas kernels for 10%

profile of v7, /device:TPU:6, one launch (start us, length us, event | category | flops | bytes accessed | tf_op | source)
XLA Modules:
  0.0 80.0 jit_solution(14283495818848779985)
XLA Ops:
  0.0 2.0 %shard_map.64 = bf16[32,3,24,128]{3,2,1,0:T(8,128)(2,1)} custom-call(bf16[1,24,4096]{2,1,0:T(8,128)(2,1)} %q_hbm.1, bf16[1,24,4096]{2,1,0:T(8,128)(2,1)} %k_hbm.1, bf16[1,24,4096]{2,1,0:T(8,128)(2,1)} %v_hbm.1), custom_call_target="tpu_custom_call" | custom-call | tf_op jit(solution)/shard_map/pallas_call | solution.py:194
  2.0 31.7 %all_to_all.10 = bf16[32,3,24,128]{3,2,1,0:T(8,128)(2,1)S(1)} all-to-all(bf16[32,3,24,128]{3,2,1,0:T(8,128)(2,1)} %shard_map.64), channel_id=1, replica_groups=mesh['x'=4,'y_hi'=2,'y_lo'=4,'z'=8,'core'=2] {'y_lo','z'}, dimensions={0} | all-to-all | bytes 1179648 | tf_op jit(solution)/shard_map/all_to_all | solution.py:181
  33.8 4.4 %collective-permute-start = (bf16[2,768,128]{2,1,0:T(8,128)(2,1)S(1)}, bf16[2,768,128]{2,1,0:T(8,128)(2,1)S(1)}, u32[]{:S(2)}, u32[]{:S(2)}) collective-permute-start(bf16[2,768,128]{2,1,0:T(8,128)(2,1)S(1)} %bitcast.12), channel_id=1, source_target_pairs={{0,112},{16,96},{32,80},{48,64},{64,176},{80,160},{96,144},{112,12... | collective-permute-start | bytes 1179656 | tf_op jit(solution)/shard_map/ppermute | solution.py:178
  38.3 2.7 %collective-permute-start.1 = (bf16[768,128]{1,0:T(8,128)(2,1)S(1)}, bf16[768,128]{1,0:T(8,128)(2,1)S(1)}, u32[]{:S(2)}, u32[]{:S(2)}) collective-permute-start(bf16[768,128]{1,0:T(8,128)(2,1)S(1)} %bitcast.8), channel_id=1, source_target_pairs={{128,0},{192,64},{256,128},{320,192},{384,256},{448,320},{129,1},{... | collective-permute-start | bytes 589832 | tf_op jit(solution)/shard_map/ppermute | solution.py:185
  41.0 2.4 %all_gather.9.kv_ref = bf16[2,2,768,128]{3,2,1,0:T(8,128)(2,1)S(1)} all-gather(bf16[1,2,768,128]{3,2,1,0:T(8,128)(2,1)S(1)} %bitcast.13), channel_id=1, replica_groups=mesh['x'=4,'y_hi'=2,'y_lo'=4,'z'=8,'core'=2] {'core'}, dimensions={0}, use_global_device_ids=true | all-gather | bytes 1179648 | tf_op jit(solution)/shard_map/all_gather | solution.py:191
  43.4 0.0 copy-start
  43.4 0.0 copy-start.1
  43.4 0.0 copy-start.2
  43.4 1.6 %collective-permute-done.1.q_ref = bf16[768,128]{1,0:T(8,128)(2,1)S(1)} collective-permute-done((bf16[768,128]{1,0:T(8,128)(2,1)S(1)}, bf16[768,128]{1,0:T(8,128)(2,1)S(1)}, u32[]{:S(2)}, u32[]{:S(2)}) %collective-permute-start.1) | collective-permute-done | bytes 196640 | tf_op jit(solution)/shard_map/ppermute | solution.py:185
  45.0 2.4 %shard_map.67 = bf16[800,128]{1,0:T(8,128)(2,1)S(1)} custom-call(bf16[768,128]{1,0:T(8,128)(2,1)S(1)} %collective-permute-done.1.q_ref, bf16[2,2,768,128]{3,2,1,0:T(8,128)(2,1)S(1)} %all_gather.9.kv_ref), custom_call_target="tpu_custom_call" | custom-call | flops 1024 | bytes 1024 | tf_op jit(solution)/shard_map/pallas_call | solution.py:155
  47.4 1.3 %collective-permute-start.2 = (bf16[800,128]{1,0:T(8,128)(2,1)S(1)}, bf16[800,128]{1,0:T(8,128)(2,1)S(1)}, u32[]{:S(2)}, u32[]{:S(2)}) collective-permute-start(bf16[800,128]{1,0:T(8,128)(2,1)S(1)} %shard_map.67), channel_id=1, source_target_pairs={{0,128},{64,192},{128,256},{192,320},{256,384},{320,448},{1,129},{... | collective-permute-start | bytes 614408 | tf_op jit(solution)/shard_map/ppermute | solution.py:185
  48.7 0.0 copy-done
  48.7 0.0 copy-done.1
  48.7 0.0 copy-done.2
  48.7 3.0 %shard_map.65 = (f32[768,128]{1,0:T(8,128)S(1)}, f32[768,128]{1,0:T(8,128)S(1)}, f32[768,128]{1,0:T(8,128)S(1)}, f32[24,128]{1,0:T(8,128)S(1)}) custom-call(s32[8,8]{1,0:T(8,128)S(1)} %copy-done.1, s32[8]{0:T(128)S(1)} %copy-done.2, f32[8,4096]{1,0:T(8,128)S(1)} %copy-done, bf16[768,128]{1,0:T(8,128)(2,1)S(1)} %bitcast.9, ...), custom_call_target="tpu_custom_call" | custom-call | flops 1024 | bytes 1024 | tf_op jit(solution)/shard_map/pallas_call | solution.py:155
  51.7 4.5 %collective-permute-done = bf16[2,768,128]{2,1,0:T(8,128)(2,1)S(1)} collective-permute-done((bf16[2,768,128]{2,1,0:T(8,128)(2,1)S(1)}, bf16[2,768,128]{2,1,0:T(8,128)(2,1)S(1)}, u32[]{:S(2)}, u32[]{:S(2)}) %collective-permute-start) | collective-permute-done | bytes 393248 | tf_op jit(solution)/shard_map/ppermute | solution.py:178
  56.2 2.4 %all-gather = bf16[4,768,128]{2,1,0:T(8,128)(2,1)S(1)} all-gather(bf16[2,768,128]{2,1,0:T(8,128)(2,1)S(1)} %collective-permute-done), channel_id=2, replica_groups=mesh['x'=4,'y_hi'=2,'y_lo'=4,'z'=8,'core'=2] {'core'}, dimensions={0}, use_global_device_ids=true | all-gather | bytes 1179648 | tf_op jit(solution)/shard_map/all_gather | solution.py:191
  58.6 2.6 %shard_map.66 = (f32[768,128]{1,0:T(8,128)S(1)}, f32[768,128]{1,0:T(8,128)S(1)}, f32[768,128]{1,0:T(8,128)S(1)}) custom-call(f32[24,128]{1,0:T(8,128)S(1)} %get-tuple-element.12.aux_ref, bf16[768,128]{1,0:T(8,128)(2,1)S(1)} %bitcast.10, bf16[2,2,768,128]{3,2,1,0:T(8,128)(2,1)S(1)} %bitcast.7, f32[768,128]{1,0:T(8,128)S(1)} %get-tuple-element.13.m_in, ...), custom_call_target="tpu_custom_call" | custom-call | flops 1024 | bytes 1024 | tf_op jit(solution)/shard_map/pallas_call | solution.py:155
  61.2 0.0 collective-permute-done.2.part_ref
  61.2 0.3 shard_map.68
  61.5 17.7 %all_to_all.11.in_ref = bf16[32,24,128]{2,1,0:T(8,128)(2,1)S(1)} all-to-all(bf16[32,24,128]{2,1,0:T(8,128)(2,1)S(1)} %bitcast.11), channel_id=1, replica_groups=mesh['x'=4,'y_hi'=2,'y_lo'=4,'z'=8,'core'=2] {'y_lo','z'}, dimensions={0} | all-to-all | bytes 393216 | tf_op jit(solution)/shard_map/all_to_all | solution.py:181
  79.2 0.7 shard_map.69
  (3 shorter events, 0.1 us)
Async XLA Ops:
  33.8 22.4 %collective-permute-start = (bf16[2,768,128]{2,1,0:T(8,128)(2,1)S(1)}, bf16[2,768,128]{2,1,0:T(8,128)(2,1)S(1)}, u32[]{:S(2)}, u32[]{:S(2)}) collective-permute-start(bf16[2,768,128]{2,1,0:T(8,128)(2,1)S(1)} %bitcast.12), channel_id=1, source_target_pairs={{0,112},{16,96},{32,80},{48,64},{64,176},{80,160},{96,144},{112,12... | collective-permute-start | bytes 1179656 | tf_op jit(solution)/shard_map/ppermute | solution.py:178
  38.3 6.7 %collective-permute-start.1 = (bf16[768,128]{1,0:T(8,128)(2,1)S(1)}, bf16[768,128]{1,0:T(8,128)(2,1)S(1)}, u32[]{:S(2)}, u32[]{:S(2)}) collective-permute-start(bf16[768,128]{1,0:T(8,128)(2,1)S(1)} %bitcast.8), channel_id=1, source_target_pairs={{128,0},{192,64},{256,128},{320,192},{384,256},{448,320},{129,1},{... | collective-permute-start | bytes 589832 | tf_op jit(solution)/shard_map/ppermute | solution.py:185
  43.4 5.3 %copy-start = (f32[8,4096]{1,0:T(8,128)S(1)}, f32[8,4096]{1,0:T(8,128)}, u32[]{:S(2)}) copy-start(f32[8,4096]{1,0:T(8,128)} %gate_ref.1) | copy-start | bytes 393220
  43.4 5.3 %copy-start.1 = (s32[8,8]{1,0:T(8,128)S(1)}, s32[8,8]{1,0:T(8,128)}, u32[]{:S(2)}) copy-start(s32[8,8]{1,0:T(8,128)} %mask_ref.1) | copy-start | bytes 772
  43.4 5.3 %copy-start.2 = (s32[8]{0:T(128)S(1)}, s32[8]{0:T(128)}, u32[]{:S(2)}) copy-start(s32[8]{0:T(128)} %level_ref.1) | copy-start | bytes 100
  47.4 13.8 %collective-permute-start.2 = (bf16[800,128]{1,0:T(8,128)(2,1)S(1)}, bf16[800,128]{1,0:T(8,128)(2,1)S(1)}, u32[]{:S(2)}, u32[]{:S(2)}) collective-permute-start(bf16[800,128]{1,0:T(8,128)(2,1)S(1)} %shard_map.67), channel_id=1, source_target_pairs={{0,128},{64,192},{128,256},{192,320},{256,384},{320,448},{1,129},{... | collective-permute-start | bytes 614408 | tf_op jit(solution)/shard_map/ppermute | solution.py:185
